TPU v7x, 256 devices: a whole 4x4x8 slice. The times are simulated.
256 devices in a mesh: slab: 64 (over z, x, core), pencil: 4 (over y).
Axes of the slice: x: 4, y: 4, z: 8, core: 2. Of those that a mesh axis runs over, the one named last changes fastest.
Arguments:
- atom_cell: int32 [3, 2097152], P(None, ('slab', 'pencil')), may hold values from 0 to 511, as said below
- charge: float32 [2097152], P(('slab', 'pencil')), may hold values from -4 to 4
Outputs:
- potential: float32 [512, 128, 512], P('slab', 'pencil')
- forces: float32 [3, 2097152], P(None, ('slab', 'pencil'))
Inputs may be any that keep to these rules, and one draw needn't show every extreme that they name: `atom_cell`: the atoms of rows b * 8192 to (b + 1) * 8192 - 1, with b = s * 4 + r, lie in z planes s * 8 to (s + 1) * 8 - 1 and y rows r * 32 to (r + 1) * 32 - 1. Row 0 is at cell (0, 0, 0) and the last row at cell (511, 127, 511).
All inputs are finite; a program needn't handle non-finite values.
Results may differ from a plain program's by a relative error of at most 0.0003.
Values sent between devices are 32-bit elements; how exact they have to be, the bound alone decides.
No kernel may reach another device: no remote copies, remote signals or barrier semaphores. Data moves between devices by JAX's collectives and lax.ppermute only.
A program may use at most 128 MiB of HBM per device.

v0:
```python
from functools import partial
import math

import jax
import jax.numpy as jnp
from jax import lax
from jax.sharding import PartitionSpec as P

CZ = 8
CY = 32
NX = 512
LEVELS = 5
RADIUS = 2
F = 32


def extended(cells, sides, width):
    for axis, dim in sides:
        count = lax.axis_size(axis)
        ends = count - 1
        head = lax.slice_in_dim(cells, 0, width, axis=dim)
        tail = lax.slice_in_dim(cells, cells.shape[dim] - width, cells.shape[dim], axis=dim)
        cells = jnp.concatenate(
            [
                lax.ppermute(tail, axis, [(i, (i + 1) % count) for i in range(ends)]),
                cells,
                lax.ppermute(head, axis, [((i + 1) % count, i) for i in range(ends)]),
            ],
            axis=dim,
        )
    return cells


def partner(value, axis, stride):
    mask = 2**stride
    pairs = [(source, source ^ mask) for source in range(lax.axis_size(axis))]
    return lax.ppermute(value, axis, pairs)


def kernel_weight(step_z, step_y, step_x):
    squared = step_z * step_z + step_y * step_y + step_x * step_x
    return 1.0 / math.sqrt(squared + 0.25) - 1.0 / math.sqrt(squared + 4.0)


def level_weight(scale, step_z, step_y, step_x):
    squared = step_z * step_z + step_y * step_y + step_x * step_x
    return scale * (1.0 / math.sqrt(squared + 1.0) - 1.0 / math.sqrt(squared + 4.0))


def short_field(padded, plane_count, row_count, row_length, radius_cells, weight_of):
    accumulated = jnp.zeros((plane_count, row_count, row_length), jnp.float32)
    for step_z in range(-radius_cells, radius_cells + 1):
        for step_y in range(-radius_cells, radius_cells + 1):
            for step_x in range(-radius_cells, radius_cells + 1):
                corner_z = radius_cells + step_z
                corner_y = radius_cells + step_y
                corner_x = radius_cells + step_x
                accumulated = (
                    accumulated
                    + weight_of(step_z, step_y, step_x)
                    * padded[
                        corner_z : corner_z + plane_count,
                        corner_y : corner_y + row_count,
                        corner_x : corner_x + row_length,
                    ]
                )
    return accumulated


def restrict(grid):
    planes, rows, length = grid.shape
    return grid.reshape(planes // 2, 2, rows // 2, 2, length // 2, 2).sum(axis=(1, 3, 5))


def restrict_plane(plane):
    rows, length = plane.shape
    return plane.reshape(rows // 2, 2, length // 2, 2).sum(axis=(1, 3))


def interp_matrix(fine_ids, level_count, factor, first_col, width):
    numerator = jnp.clip(2 * fine_ids + 1 - factor, 0, 2 * factor * (level_count - 1))
    lower_index = jnp.minimum(numerator // (2 * factor), level_count - 2)
    fraction = (numerator - lower_index * 2 * factor).astype(jnp.float32) / (2.0 * factor)
    local_index = lower_index - first_col
    columns = jnp.arange(width, dtype=jnp.int32)
    low_part = jnp.where(columns[None, :] == local_index[:, None], 1.0 - fraction[:, None], 0.0)
    high_part = jnp.where(columns[None, :] == local_index[:, None] + 1, fraction[:, None], 0.0)
    return low_part + high_part


def to_fine(field, counts, factor, plane_ids, line_ids, column_ids, first_z, first_y):
    width_z, width_y, width_x = field.shape
    along_z = interp_matrix(plane_ids, counts[0], factor, first_z, width_z)
    along_y = interp_matrix(line_ids, counts[1], factor, first_y, width_y)
    along_x = interp_matrix(column_ids, counts[2], factor, 0, width_x)
    section = jnp.einsum("fa,abc->fbc", along_z, field, precision=lax.Precision.HIGHEST)
    section = jnp.einsum("fb,abc->afc", along_y, section, precision=lax.Precision.HIGHEST)
    return jnp.einsum("fc,abc->abf", along_x, section, precision=lax.Precision.HIGHEST)


def top_coords(cell_ids, top_y, top_x):
    return (cell_ids // (top_y * top_x), cell_ids // top_x % top_y, cell_ids % top_x)


def top_potential(targets, charges_flat, top_z, top_y, top_x, strength):
    sources = jnp.arange(top_z * top_y * top_x, dtype=jnp.int32)
    target_xyz = top_coords(targets, top_y, top_x)
    source_xyz = top_coords(sources, top_y, top_x)
    distance = jnp.ones((targets.shape[0], sources.shape[0]), jnp.float32)
    for component in range(3):
        offset = (target_xyz[component][:, None] - source_xyz[component][None, :]).astype(
            jnp.float32
        )
        distance = distance + offset * offset
    kernel = strength / jnp.sqrt(distance)
    return jnp.dot(kernel, charges_flat, precision=lax.Precision.HIGHEST)


def gradient_along(padded, direction, plane_count, row_count, row_length):

    def shifted(offset_cells):
        corner = [2, 2, 2]
        corner[direction] = corner[direction] + offset_cells
        return padded[
            corner[0] : corner[0] + plane_count,
            corner[1] : corner[1] + row_count,
            corner[2] : corner[2] + row_length,
        ]

    return (8.0 * (shifted(1) - shifted(-1)) - (shifted(2) - shifted(-2))) / 12.0


def fold_copies(block):
    while block.shape[1] > 1:
        block = 0.5 * (block[:, 0::2] + block[:, 1::2])
    return block[:, 0]


def body(atom_cell, charge):
    slab_pos = lax.axis_index("slab")
    pencil_pos = lax.axis_index("pencil")
    slabs = lax.axis_size("slab")
    pencils = lax.axis_size("pencil")
    atom_total = charge.shape[0]
    row_cells = CZ * CY
    plane_row = (atom_cell[0] - slab_pos * CZ) * CY + (atom_cell[1] - pencil_pos * CY)
    column_of = atom_cell[2]
    block_atoms = math.gcd(atom_total, 512)
    block_count = atom_total // block_atoms
    row_blocks = plane_row.reshape(block_count, block_atoms)
    column_blocks = column_of.reshape(block_count, block_atoms)
    charge_blocks = charge.reshape(block_count, block_atoms)
    row_range = jnp.arange(row_cells, dtype=jnp.int32)
    column_range = jnp.arange(NX, dtype=jnp.int32)

    def deposit(total, block):
        rows_here, columns_here, charges_here = block
        row_table = (rows_here[:, None] == row_range[None, :]).astype(jnp.float32)
        column_table = jnp.where(
            columns_here[:, None] == column_range[None, :], charges_here[:, None], 0.0
        )
        added = jnp.dot(row_table.T, column_table, precision=lax.Precision.HIGHEST)
        return (total + added, None)

    charge_grid, _ = lax.scan(
        deposit, jnp.zeros((row_cells, NX), jnp.float32), (row_blocks, column_blocks, charge_blocks)
    )
    charge_grid = charge_grid.reshape(CZ, CY, NX)
    plane_ids = slab_pos * CZ + jnp.arange(CZ, dtype=jnp.int32)
    line_ids = pencil_pos * CY + jnp.arange(CY, dtype=jnp.int32)
    column_ids = jnp.arange(NX, dtype=jnp.int32)
    plane_level = CZ.bit_length() - 1
    rimmed = extended(charge_grid, (("slab", 0), ("pencil", 1)), RADIUS)
    padded = jnp.pad(rimmed, ((0, 0), (0, 0), (RADIUS, RADIUS)))
    potential = short_field(padded, CZ, CY, NX, RADIUS, kernel_weight)
    level_charge = charge_grid
    for level in range(1, plane_level):
        level_charge = restrict(level_charge)
        level_z, level_y, level_x = level_charge.shape
        cycle = extended(level_charge, (("slab", 0), ("pencil", 1)), RADIUS)
        cycle = jnp.pad(cycle, ((0, 0), (0, 0), (RADIUS, RADIUS)))
        field = short_field(
            cycle, level_z, level_y, level_x, RADIUS, partial(level_weight, 1.0 / 2**level)
        )
        framed = extended(field, (("slab", 0), ("pencil", 1)), 1)
        counts = (level_z * slabs, level_y * pencils, level_x)
        potential = potential + to_fine(
            framed,
            counts,
            2**level,
            plane_ids,
            line_ids,
            column_ids,
            slab_pos * level_z - 1,
            pencil_pos * level_y - 1,
        )
    own_plane = restrict(level_charge)[0]
    pieces = [own_plane]
    merged = own_plane
    for level_bit in range(LEVELS - plane_level):
        partial_plane = restrict_plane(merged)
        merged = partial_plane + partner(partial_plane, "slab", level_bit)
        pieces.append(merged)
    packed = jnp.concatenate([piece.reshape(1, -1) for piece in pieces], axis=1)
    gathered = lax.all_gather(packed, ("slab", "pencil"), axis=0, tiled=True)
    coarse = []
    offset = 0
    for step, piece in enumerate(pieces):
        rows, length = piece.shape
        group = 2**step
        block = gathered[:, offset : offset + rows * length].reshape(
            slabs // group, group, pencils, rows, length
        )
        grid = fold_copies(block)
        coarse.append(grid.reshape(slabs // group, pencils * rows, length))
        offset = offset + rows * length
    for step in range(LEVELS - plane_level):
        level = plane_level + step
        grid = coarse[step]
        level_z, level_y, level_x = grid.shape
        field = short_field(
            jnp.pad(grid, RADIUS),
            level_z,
            level_y,
            level_x,
            RADIUS,
            partial(level_weight, 1.0 / 2**level),
        )
        potential = potential + to_fine(
            field, field.shape, 2**level, plane_ids, line_ids, column_ids, 0, 0
        )
    top_grid = coarse[-1]
    top_z, top_y, top_x = top_grid.shape
    charges_flat = top_grid.reshape(top_z * top_y * top_x)
    top_total = top_z * top_y * top_x
    strength = 1.0 / F
    block_rows = math.gcd(top_total, 512)
    target_blocks = jnp.arange(top_total, dtype=jnp.int32).reshape(
        top_total // block_rows, block_rows
    )
    top_field = lax.map(
        lambda targets: top_potential(targets, charges_flat, top_z, top_y, top_x, strength),
        target_blocks,
    )
    top_field = top_field.reshape(top_z, top_y, top_x)
    potential = potential + to_fine(
        top_field, top_field.shape, F, plane_ids, line_ids, column_ids, 0, 0
    )
    rimmed_field = extended(potential, (("slab", 0), ("pencil", 1)), 2)
    padded_field = jnp.pad(rimmed_field, ((0, 0), (0, 0), (2, 2)))
    gradients = jnp.stack(
        [gradient_along(padded_field, direction, CZ, CY, NX) for direction in range(3)]
    ).reshape(3, row_cells, NX)

    def pick(block):
        rows_here, columns_here, charges_here = block
        row_table = (rows_here[:, None] == row_range[None, :]).astype(jnp.float32)
        column_table = (columns_here[:, None] == column_range[None, :]).astype(jnp.float32)
        picked_rows = jnp.einsum(
            "ar,drx->adx", row_table, gradients, precision=lax.Precision.HIGHEST
        )
        at_cell = jnp.sum(picked_rows * column_table[:, None, :], axis=2)
        return -charges_here[:, None] * at_cell

    picked = lax.map(pick, (row_blocks, column_blocks, charge_blocks))
    forces = picked.reshape(atom_total, 3).T
    return (potential, forces)


def solution(mesh):
    return jax.shard_map(
        body,
        mesh=mesh,
        in_specs=(P(None, ("slab", "pencil")), P(("slab", "pencil"))),
        out_specs=(P("slab", "pencil", None), P(None, ("slab", "pencil"))),
        check_vma=False,
    )
```

profile of v0, /device:TPU:136, one launch (start us, length us, event | category | flops | bytes accessed | tf_op | source)
XLA Modules:
  0.0 340.9 jit_solution(7631364035570809709)
XLA Ops:
  0.7 1.3 slice_reduce_fusion
  2.7 18.5 %while.37 = (s32[]{:T(128)}, f32[256,512]{1,0:T(8,128)S(1)}, s32[16,512]{1,0:T(8,128)S(1)}, s32[16,512]{1,0:T(8,128)S(1)}, f32[16,512]{1,0:T(8,128)S(1)}, /*index=5*/s32[]{:T(128)}, s32[]{:T(128)}) while((s32[]{:T(128)}, f32[256,512]{1,0:T(8,128)S(1)}, s32[16,512]{1,0:T(8,128)S(1)}, s32[16,512]{1,0:T(8,128)S(1)}, ...), condition=%wide.region_1.2_spmd.clone, body=%wide.region_0.1_spmd.clone.sunk | while | flops 806223872 | bytes 1067103 | solution.py:165
  21.2 34.9 %reshape_reshape.3 = f32[4,2,16,2,256,2]{5,4,3,2,1,0:T(8,128)} reshape(f32[256,512]{1,0:T(8,128)S(1)} %get-tuple-element.168) | data formatting | bytes 1048576 | tf_op jit(solution)/shard_map/reshape;reshape | solution.py:72
  56.1 11.6 %fusion.1179 = (f32[16,256]{1,0:T(8,128)S(1)}, f32[4,16,256]{2,1,0:T(8,128)S(1)}) fusion(f32[4,2,16,2,256,2]{5,4,3,2,1,0:T(8,128)} %reshape_reshape.3), kind=kLoop, calls=%fused_computation.2072 | loop fusion | flops 241664 | bytes 606208 | tf_op jit(solution)/shard_map/reduce_sum | solution.py:72
  67.7 5.5 %reshape.787 = f32[2,2,8,2,128,2]{5,4,3,2,1,0:T(8,128)} reshape(f32[4,16,256]{2,1,0:T(8,128)S(1)} %get-tuple-element.209) | data formatting | bytes 131072 | tf_op jit(solution)/shard_map/reshape | solution.py:72
  73.2 2.5 reduce_sum.66
  75.7 1.9 collective-permute-start.12
  77.7 7.0 %collective-permute-start.13 = (f32[2,8,128]{2,1,0:T(8,128)S(1)}, f32[2,8,128]{2,1,0:T(8,128)S(1)}, u32[]{:S(2)}, u32[]{:S(2)}) collective-permute-start(f32[2,8,128]{2,1,0:T(8,128)S(1)} %reduce_sum.66), channel_id=1, source_target_pairs={{4,0},{8,4},{12,8},{16,12},{20,16},{24,20},{28,24},{32,28},{36,32}... | collective-permute-start | bytes 24584 | tf_op jit(solution)/shard_map/ppermute | solution.py:27
  86.5 2.4 collective-permute-start.4
  88.9 6.5 %collective-permute-start.5 = (f32[2,16,256]{2,0,1:T(2,128)S(1)}, f32[2,16,256]{2,0,1:T(2,128)S(1)}, u32[]{:S(2)}, u32[]{:S(2)}) collective-permute-start(f32[2,16,256]{2,0,1:T(2,128)S(1)} %get-tuple-element.282), channel_id=1, source_target_pairs={{4,0},{8,4},{12,8},{16,12},{20,16},{24,20},{28,24},{32,28},{36,32}... | collective-permute-start | bytes 98312 | tf_op jit(solution)/shard_map/ppermute | solution.py:27
  96.6 3.4 %collective-permute-done.21 = f32[1,16]{1,0:T(1,128)S(1)} collective-permute-done((f32[1,16]{1,0:T(1,128)S(1)}, f32[1,16]{1,0:T(1,128)S(1)}, u32[]{:S(2)}, u32[]{:S(2)}) %collective-permute-start.21) | collective-permute-done | bytes 96 | tf_op jit(solution)/shard_map/ppermute | solution.py:37
  100.1 1.9 collective-permute-start
  102.1 66.2 %all-gather = f32[256,1,336]{2,1,0:T(1,128)S(1)} all-gather(f32[1,1,336]{2,1,0:T(1,128)S(1)} %maximum_bitcast_fusion), channel_id=1, replica_groups=mesh['slab'=64,'pencil'=4] {'slab','pencil'}, dimensions={0}, use_global_device_ids=true | all-gather | bytes 345408 | tf_op jit(solution)/shard_map/all_gather | solution.py:205
  169.0 13.9 %fusion.343 = f32[64,16,64]{2,1,0:T(8,128)S(1)} fusion(f32[64,16,64]{2,1,0:T(8,128)S(1)} %reshape_squeeze_reshape.3), kind=kLoop, calls=%fused_computation.659 | loop fusion | flops 16318464 | bytes 524288 | tf_op jit(solution)/shard_map/add | solution.py:59
  183.5 6.0 %while.35 = (s32[]{:T(128)}, f32[2,512]{1,0:T(2,128)S(1)}, s32[2,512]{1,0:T(2,128)S(1)}, f32[1024]{0:T(1024)S(1)}, s32[]{:T(128)}, /*index=5*/s32[]{:T(128)}) while((s32[]{:T(128)}, f32[2,512]{1,0:T(2,128)S(1)}, s32[2,512]{1,0:T(2,128)S(1)}, f32[1024]{0:T(1024)S(1)}, s32[]{:T(128)}, /*index=5*/s32[]{:T(128)}) %tuple.130), condition=%wide.region_11.12_spmd, body=%wide.region_10.11_spmd.sunk | while | flops 13159426 | bytes 53325 | solution.py:241
  183.6 2.9 fusion.1203
  186.6 2.9 fusion.1203
  190.3 4.3 %fusion.731 = f32[8,8,32]{2,0,1:T(8,128)S(1)} fusion(f32[32,8,32]{2,0,1:T(8,128)S(1)} %copy.72, f32[8]{0:T(128)S(1)} %get-tuple-element.308, s32[8]{0:T(128)S(1)} %get-tuple-element.321, f32[8]{0:T(128)S(1)} %get-tuple-element.319, s32[8]{0:T(128)S(1)} %get-tuple-element.310), kind=kOutput, calls=%fused_computation.1194 | convolution fusion | flops 2827520 | bytes 41088 | tf_op jit(solution)/shard_map/fa,abc->fbc/dot_general | solution.py:96
  195.2 2.5 collective-permute-start.14
  197.7 3.3 collective-permute-start.15
  201.3 2.0 collective-permute-done.15
  203.7 1.9 collective-permute-start.16
  205.6 7.0 %collective-permute-start.17 = (f32[1,8,128]{2,1,0:T(8,128)S(1)}, f32[1,8,128]{2,1,0:T(8,128)S(1)}, u32[]{:S(2)}, u32[]{:S(2)}) collective-permute-start(f32[1,8,128]{2,1,0:T(8,128)S(1)} %get-tuple-element.290), channel_id=1, source_target_pairs={{4,0},{8,4},{12,8},{16,12},{20,16},{24,20},{28,24},{32,28},{36,32}... | collective-permute-start | bytes 12296 | tf_op jit(solution)/shard_map/ppermute | solution.py:27
  212.9 1.9 collective-permute-start.1
  214.8 3.9 %collective-permute-start.18 = (f32[4,1,128]{2,1,0:T(1,128)S(1)}, f32[4,1,128]{2,1,0:T(1,128)S(1)}, u32[]{:S(2)}, u32[]{:S(2)}) collective-permute-start(f32[4,1,128]{2,1,0:T(1,128)S(1)} %get-tuple-element.287), channel_id=1, source_target_pairs={{0,1},{1,2},{2,3},{4,5},{5,6},{6,7},{8,9},{9,10},{10,11},{12,13},{... | collective-permute-start | bytes 6152 | tf_op jit(solution)/shard_map/ppermute | solution.py:25
  218.8 1.9 collective-permute-start.19
  220.7 3.9 %collective-permute-start.6 = (f32[8,2,256]{2,0,1:T(8,128)S(1)}, f32[8,2,256]{2,0,1:T(8,128)S(1)}, u32[]{:S(2)}, u32[]{:S(2)}) collective-permute-start(f32[8,2,256]{2,0,1:T(8,128)S(1)} %get-tuple-element.275), channel_id=1, source_target_pairs={{0,1},{1,2},{2,3},{4,5},{5,6},{6,7},{8,9},{9,10},{10,11},{12,13},{... | collective-permute-start | bytes 49160 | tf_op jit(solution)/shard_map/ppermute | solution.py:25
  224.7 1.9 collective-permute-start.7
  226.6 3.7 %collective-permute-done.7 = f32[8,2,256]{2,0,1:T(8,128)S(1)} collective-permute-done((f32[8,2,256]{2,0,1:T(8,128)S(1)}, f32[8,2,256]{2,0,1:T(8,128)S(1)}, u32[]{:S(2)}, u32[]{:S(2)}) %collective-permute-start.7) | collective-permute-done | bytes 16416 | tf_op jit(solution)/shard_map/ppermute | solution.py:27
  230.6 2.7 fusion.757
  233.4 1.9 collective-permute-start.8
  235.3 7.0 %collective-permute-start.9 = (f32[1,16,256]{2,0,1:T(1,128)S(1)}, f32[1,16,256]{2,0,1:T(1,128)S(1)}, u32[]{:S(2)}, u32[]{:S(2)}) collective-permute-start(f32[1,16,256]{2,0,1:T(1,128)S(1)} %get-tuple-element.280), channel_id=1, source_target_pairs={{4,0},{8,4},{12,8},{16,12},{20,16},{24,20},{28,24},{32,28},{36,32}... | collective-permute-start | bytes 49160 | tf_op jit(solution)/shard_map/ppermute | solution.py:27
  242.5 1.2 collective-permute-done.9
  243.7 1.9 collective-permute-start.10
  245.6 4.1 %collective-permute-start.11 = (f32[6,1,256]{2,0,1:T(8,128)S(1)}, f32[6,1,256]{2,0,1:T(8,128)S(1)}, u32[]{:S(2)}, u32[]{:S(2)}) collective-permute-start(f32[6,1,256]{2,0,1:T(8,128)S(1)} %get-tuple-element.278), channel_id=1, source_target_pairs={{1,0},{2,1},{3,2},{5,4},{6,5},{7,6},{9,8},{10,9},{11,10},{13,12},{... | collective-permute-start | bytes 18440 | tf_op jit(solution)/shard_map/ppermute | solution.py:27
  250.1 1.1 collective-permute-done.11
  251.6 1.9 collective-permute-start.2
  253.5 3.9 %collective-permute-start.3 = (f32[12,2,512]{2,1,0:T(2,128)S(1)}, f32[12,2,512]{2,1,0:T(2,128)S(1)}, u32[]{:S(2)}, u32[]{:S(2)}) collective-permute-start(f32[12,2,512]{2,1,0:T(2,128)S(1)} %get-tuple-element.268), channel_id=1, source_target_pairs={{1,0},{2,1},{3,2},{5,4},{6,5},{7,6},{9,8},{10,9},{11,10},{13,12},{... | collective-permute-start | bytes 147464 | tf_op jit(solution)/shard_map/ppermute | solution.py:27
  257.9 1.6 collective-permute-done.3
  260.3 10.6 %convolution_add_fusion.5 = f32[8,32,512]{2,1,0:T(8,128)S(1)} fusion(f32[8,32,256]{2,1,0:T(8,128)S(1)} %convolution_bitcast_fusion, f32[12,36,516]{2,1,0:T(8,128)S(1)} %select_maximum_fusion.4, f32[12,34,512]{2,1,0:T(8,128)S(1)} %get-tuple-element.266, f32[2,32,512]{2,1,0:T(8,128)S(1)} %collective-permute-done.1, f32[8,32,512]{2,1,0:T(8,128)S(1)} %bitcast.123, ...), kind=kOutput, calls=%fused_computation.342 | convolution fusion | flops 436600832 | bytes 64495616 | tf_op jit(solution)/shard_map/fc,abc->abf/dot_general | solution.py:98
  270.9 1.5 convolution_add_fusion.4
  274.4 4.6 %collective-permute-start.22 = (f32[2,32,512]{2,1,0:T(8,128)S(1)}, f32[2,32,512]{2,1,0:T(8,128)S(1)}, u32[]{:S(2)}, u32[]{:S(2)}) collective-permute-start(f32[2,32,512]{2,1,0:T(8,128)S(1)} %get-tuple-element.270), channel_id=1, source_target_pairs={{4,0},{8,4},{12,8},{16,12},{20,16},{24,20},{28,24},{32,28},{36,32}... | collective-permute-start | bytes 393224 | tf_op jit(solution)/shard_map/ppermute | solution.py:27
  279.1 1.9 collective-permute-start.23
  281.6 7.1 %collective-permute-done.23 = f32[2,32,512]{2,1,0:T(8,128)S(1)} collective-permute-done((f32[2,32,512]{2,1,0:T(8,128)S(1)}, f32[2,32,512]{2,1,0:T(8,128)S(1)}, u32[]{:S(2)}, u32[]{:S(2)}) %collective-permute-start.23) | collective-permute-done | bytes 131104 | tf_op jit(solution)/shard_map/ppermute | solution.py:25
  288.7 3.6 %collective-permute-start.24 = (f32[12,2,512]{2,1,0:T(2,128)S(1)}, f32[12,2,512]{2,1,0:T(2,128)S(1)}, u32[]{:S(2)}, u32[]{:S(2)}) collective-permute-start(f32[12,2,512]{2,1,0:T(2,128)S(1)} %get-tuple-element.264), channel_id=1, source_target_pairs={{1,0},{2,1},{3,2},{5,4},{6,5},{7,6},{9,8},{10,9},{11,10},{13,12},{... | collective-permute-start | bytes 147464 | tf_op jit(solution)/shard_map/ppermute | solution.py:27
  292.3 2.2 collective-permute-start.25
  294.9 3.4 %collective-permute-done.25 = f32[12,2,512]{2,1,0:T(2,128)S(1)} collective-permute-done((f32[12,2,512]{2,1,0:T(2,128)S(1)}, f32[12,2,512]{2,1,0:T(2,128)S(1)}, u32[]{:S(2)}, u32[]{:S(2)}) %collective-permute-start.25) | collective-permute-done | bytes 49184 | tf_op jit(solution)/shard_map/ppermute | solution.py:25
  300.3 40.4 %while.36 = (s32[]{:T(128)}, f32[16,512,3]{1,2,0:T(4,128)}, f32[16,512]{1,0:T(8,128)S(1)}, s32[16,512]{1,0:T(8,128)S(1)}, f32[3,256,512]{1,2,0:T(8,128)S(1)}, /*index=5*/s32[16,512]{1,0:T(8,128)S(1)}, s32[]{:T(128)}) while((s32[]{:T(128)}, f32[16,512,3]{1,2,0:T(4,128)}, f32[16,512]{1,0:T(8,128)S(1)}, s32[16,512]{1,0:T(8,128)S(1)}, ...), condition=%wide.region_14.15_spmd.clone, body=%wide.region_12.14_spmd.clone.sunk | while | flops 2418147840 | bytes 3709525 | solution.py:265
  300.5 1.7 multiply_reduce_fusion.2
  303.0 1.7 multiply_reduce_fusion.2
  305.5 1.7 multiply_reduce_fusion.2
  308.0 1.7 multiply_reduce_fusion.2
  310.6 1.7 multiply_reduce_fusion.2
  313.1 1.7 multiply_reduce_fusion.2
  315.6 1.7 multiply_reduce_fusion.2
  318.1 1.7 multiply_reduce_fusion.2
  320.7 1.7 multiply_reduce_fusion.2
  323.2 1.7 multiply_reduce_fusion.2
  325.7 1.7 multiply_reduce_fusion.2
  328.2 1.7 multiply_reduce_fusion.2
  330.7 1.7 multiply_reduce_fusion.2
  333.3 1.7 multiply_reduce_fusion.2
  335.8 1.7 multiply_reduce_fusion.2
  338.3 1.7 multiply_reduce_fusion.2
  (250 shorter events, 44.6 us)
Async XLA Ops:
  75.7 119.4 %collective-permute-start.12 = (f32[2,8,128]{2,1,0:T(8,128)S(1)}, f32[2,8,128]{2,1,0:T(8,128)S(1)}, u32[]{:S(2)}, u32[]{:S(2)}) collective-permute-start(f32[2,8,128]{2,1,0:T(8,128)S(1)} %reduce_sum.66), channel_id=1, source_target_pairs={{0,4},{4,8},{8,12},{12,16},{16,20},{20,24},{24,28},{28,32},{32,36}... | collective-permute-start | bytes 24584 | tf_op jit(solution)/shard_map/ppermute | solution.py:25
  77.7 117.5 %collective-permute-start.13 = (f32[2,8,128]{2,1,0:T(8,128)S(1)}, f32[2,8,128]{2,1,0:T(8,128)S(1)}, u32[]{:S(2)}, u32[]{:S(2)}) collective-permute-start(f32[2,8,128]{2,1,0:T(8,128)S(1)} %reduce_sum.66), channel_id=1, source_target_pairs={{4,0},{8,4},{12,8},{16,12},{20,16},{24,20},{28,24},{32,28},{36,32}... | collective-permute-start | bytes 24584 | tf_op jit(solution)/shard_map/ppermute | solution.py:27
  86.4 9.8 %collective-permute-start.20 = (f32[2,32]{1,0:T(2,128)S(1)}, f32[2,32]{1,0:T(2,128)S(1)}, u32[]{:S(2)}, u32[]{:S(2)}) collective-permute-start(f32[2,32]{1,0:T(2,128)S(1)} %reduce_sum.86), channel_id=1, source_target_pairs={{0,4},{4,0},{8,12},{12,8},{16,20},{20,16},{24,28},{28,24},{32,36},... | collective-permute-start | bytes 776 | tf_op jit(solution)/shard_map/ppermute | solution.py:37
  86.5 132.2 %collective-permute-start.4 = (f32[2,16,256]{2,0,1:T(2,128)S(1)}, f32[2,16,256]{2,0,1:T(2,128)S(1)}, u32[]{:S(2)}, u32[]{:S(2)}) collective-permute-start(f32[2,16,256]{2,0,1:T(2,128)S(1)} %get-tuple-element.281), channel_id=1, source_target_pairs={{0,4},{4,8},{8,12},{12,16},{16,20},{20,24},{24,28},{28,32},{32,36}... | collective-permute-start | bytes 98312 | tf_op jit(solution)/shard_map/ppermute | solution.py:25
  88.9 131.8 %collective-permute-start.5 = (f32[2,16,256]{2,0,1:T(2,128)S(1)}, f32[2,16,256]{2,0,1:T(2,128)S(1)}, u32[]{:S(2)}, u32[]{:S(2)}) collective-permute-start(f32[2,16,256]{2,0,1:T(2,128)S(1)} %get-tuple-element.282), channel_id=1, source_target_pairs={{4,0},{8,4},{12,8},{16,12},{20,16},{24,20},{28,24},{32,28},{36,32}... | collective-permute-start | bytes 98312 | tf_op jit(solution)/shard_map/ppermute | solution.py:27
  96.5 3.6 %collective-permute-start.21 = (f32[1,16]{1,0:T(1,128)S(1)}, f32[1,16]{1,0:T(1,128)S(1)}, u32[]{:S(2)}, u32[]{:S(2)}) collective-permute-start(f32[1,16]{1,0:T(1,128)S(1)} %bitcast.142), channel_id=1, source_target_pairs={{0,8},{4,12},{8,0},{12,4},{16,24},{20,28},{24,16},{28,20},{32,40},... | collective-permute-start | bytes 200 | tf_op jit(solution)/shard_map/ppermute | solution.py:37
  100.1 151.4 %collective-permute-start = (f32[2,32,512]{2,1,0:T(8,128)S(1)}, f32[2,32,512]{2,1,0:T(8,128)S(1)}, u32[]{:S(2)}, u32[]{:S(2)}) collective-permute-start(f32[2,32,512]{2,1,0:T(8,128)S(1)} %bitcast.137), channel_id=1, source_target_pairs={{0,4},{4,8},{8,12},{12,16},{16,20},{20,24},{24,28},{28,32},{32,36}... | collective-permute-start | bytes 393224 | tf_op jit(solution)/shard_map/ppermute | solution.py:25
  195.2 6.1 %collective-permute-start.14 = (f32[6,2,128]{2,1,0:T(2,128)S(1)}, f32[6,2,128]{2,1,0:T(2,128)S(1)}, u32[]{:S(2)}, u32[]{:S(2)}) collective-permute-start(f32[6,2,128]{2,1,0:T(2,128)S(1)} %get-tuple-element.285), channel_id=1, source_target_pairs={{0,1},{1,2},{2,3},{4,5},{5,6},{6,7},{8,9},{9,10},{10,11},{12,13},{... | collective-permute-start | bytes 18440 | tf_op jit(solution)/shard_map/ppermute | solution.py:25
  197.7 5.5 %collective-permute-start.15 = (f32[6,2,128]{2,1,0:T(2,128)S(1)}, f32[6,2,128]{2,1,0:T(2,128)S(1)}, u32[]{:S(2)}, u32[]{:S(2)}) collective-permute-start(f32[6,2,128]{2,1,0:T(2,128)S(1)} %get-tuple-element.286), channel_id=1, source_target_pairs={{1,0},{2,1},{3,2},{5,4},{6,5},{7,6},{9,8},{10,9},{11,10},{13,12},{... | collective-permute-start | bytes 18440 | tf_op jit(solution)/shard_map/ppermute | solution.py:27
  203.7 9.2 %collective-permute-start.16 = (f32[1,8,128]{2,1,0:T(8,128)S(1)}, f32[1,8,128]{2,1,0:T(8,128)S(1)}, u32[]{:S(2)}, u32[]{:S(2)}) collective-permute-start(f32[1,8,128]{2,1,0:T(8,128)S(1)} %get-tuple-element.289), channel_id=1, source_target_pairs={{0,4},{4,8},{8,12},{12,16},{16,20},{20,24},{24,28},{28,32},{32,36}... | collective-permute-start | bytes 12296 | tf_op jit(solution)/shard_map/ppermute | solution.py:25
  205.6 9.2 %collective-permute-start.17 = (f32[1,8,128]{2,1,0:T(8,128)S(1)}, f32[1,8,128]{2,1,0:T(8,128)S(1)}, u32[]{:S(2)}, u32[]{:S(2)}) collective-permute-start(f32[1,8,128]{2,1,0:T(8,128)S(1)} %get-tuple-element.290), channel_id=1, source_target_pairs={{4,0},{8,4},{12,8},{16,12},{20,16},{24,20},{28,24},{32,28},{36,32}... | collective-permute-start | bytes 12296 | tf_op jit(solution)/shard_map/ppermute | solution.py:27
  212.9 38.7 %collective-permute-start.1 = (f32[2,32,512]{2,1,0:T(8,128)S(1)}, f32[2,32,512]{2,1,0:T(8,128)S(1)}, u32[]{:S(2)}, u32[]{:S(2)}) collective-permute-start(f32[2,32,512]{2,1,0:T(8,128)S(1)} %bitcast.136), channel_id=1, source_target_pairs={{4,0},{8,4},{12,8},{16,12},{20,16},{24,20},{28,24},{32,28},{36,32}... | collective-permute-start | bytes 393224 | tf_op jit(solution)/shard_map/ppermute | solution.py:27
  214.8 9.8 %collective-permute-start.18 = (f32[4,1,128]{2,1,0:T(1,128)S(1)}, f32[4,1,128]{2,1,0:T(1,128)S(1)}, u32[]{:S(2)}, u32[]{:S(2)}) collective-permute-start(f32[4,1,128]{2,1,0:T(1,128)S(1)} %get-tuple-element.287), channel_id=1, source_target_pairs={{0,1},{1,2},{2,3},{4,5},{5,6},{6,7},{8,9},{9,10},{10,11},{12,13},{... | collective-permute-start | bytes 6152 | tf_op jit(solution)/shard_map/ppermute | solution.py:25
  218.8 7.8 %collective-permute-start.19 = (f32[4,1,128]{2,1,0:T(1,128)S(1)}, f32[4,1,128]{2,1,0:T(1,128)S(1)}, u32[]{:S(2)}, u32[]{:S(2)}) collective-permute-start(f32[4,1,128]{2,1,0:T(1,128)S(1)} %get-tuple-element.288), channel_id=1, source_target_pairs={{1,0},{2,1},{3,2},{5,4},{6,5},{7,6},{9,8},{10,9},{11,10},{13,12},{... | collective-permute-start | bytes 6152 | tf_op jit(solution)/shard_map/ppermute | solution.py:27
  220.7 5.9 %collective-permute-start.6 = (f32[8,2,256]{2,0,1:T(8,128)S(1)}, f32[8,2,256]{2,0,1:T(8,128)S(1)}, u32[]{:S(2)}, u32[]{:S(2)}) collective-permute-start(f32[8,2,256]{2,0,1:T(8,128)S(1)} %get-tuple-element.275), channel_id=1, source_target_pairs={{0,1},{1,2},{2,3},{4,5},{5,6},{6,7},{8,9},{9,10},{10,11},{12,13},{... | collective-permute-start | bytes 49160 | tf_op jit(solution)/shard_map/ppermute | solution.py:25
  224.7 5.6 %collective-permute-start.7 = (f32[8,2,256]{2,0,1:T(8,128)S(1)}, f32[8,2,256]{2,0,1:T(8,128)S(1)}, u32[]{:S(2)}, u32[]{:S(2)}) collective-permute-start(f32[8,2,256]{2,0,1:T(8,128)S(1)} %get-tuple-element.276), channel_id=1, source_target_pairs={{1,0},{2,1},{3,2},{5,4},{6,5},{7,6},{9,8},{10,9},{11,10},{13,12},{... | collective-permute-start | bytes 49160 | tf_op jit(solution)/shard_map/ppermute | solution.py:27
  233.4 9.1 %collective-permute-start.8 = (f32[1,16,256]{2,0,1:T(1,128)S(1)}, f32[1,16,256]{2,0,1:T(1,128)S(1)}, u32[]{:S(2)}, u32[]{:S(2)}) collective-permute-start(f32[1,16,256]{2,0,1:T(1,128)S(1)} %get-tuple-element.279), channel_id=1, source_target_pairs={{0,4},{4,8},{8,12},{12,16},{16,20},{20,24},{24,28},{28,32},{32,36}... | collective-permute-start | bytes 49160 | tf_op jit(solution)/shard_map/ppermute | solution.py:25
  235.3 8.4 %collective-permute-start.9 = (f32[1,16,256]{2,0,1:T(1,128)S(1)}, f32[1,16,256]{2,0,1:T(1,128)S(1)}, u32[]{:S(2)}, u32[]{:S(2)}) collective-permute-start(f32[1,16,256]{2,0,1:T(1,128)S(1)} %get-tuple-element.280), channel_id=1, source_target_pairs={{4,0},{8,4},{12,8},{16,12},{20,16},{24,20},{28,24},{32,28},{36,32}... | collective-permute-start | bytes 49160 | tf_op jit(solution)/shard_map/ppermute | solution.py:27
  243.7 6.3 %collective-permute-start.10 = (f32[6,1,256]{2,0,1:T(8,128)S(1)}, f32[6,1,256]{2,0,1:T(8,128)S(1)}, u32[]{:S(2)}, u32[]{:S(2)}) collective-permute-start(f32[6,1,256]{2,0,1:T(8,128)S(1)} %get-tuple-element.277), channel_id=1, source_target_pairs={{0,1},{1,2},{2,3},{4,5},{5,6},{6,7},{8,9},{9,10},{10,11},{12,13},{... | collective-permute-start | bytes 18440 | tf_op jit(solution)/shard_map/ppermute | solution.py:25
  245.6 5.5 %collective-permute-start.11 = (f32[6,1,256]{2,0,1:T(8,128)S(1)}, f32[6,1,256]{2,0,1:T(8,128)S(1)}, u32[]{:S(2)}, u32[]{:S(2)}) collective-permute-start(f32[6,1,256]{2,0,1:T(8,128)S(1)} %get-tuple-element.278), channel_id=1, source_target_pairs={{1,0},{2,1},{3,2},{5,4},{6,5},{7,6},{9,8},{10,9},{11,10},{13,12},{... | collective-permute-start | bytes 18440 | tf_op jit(solution)/shard_map/ppermute | solution.py:27
  251.6 6.3 %collective-permute-start.2 = (f32[12,2,512]{2,1,0:T(2,128)S(1)}, f32[12,2,512]{2,1,0:T(2,128)S(1)}, u32[]{:S(2)}, u32[]{:S(2)}) collective-permute-start(f32[12,2,512]{2,1,0:T(2,128)S(1)} %get-tuple-element.267), channel_id=1, source_target_pairs={{0,1},{1,2},{2,3},{4,5},{5,6},{6,7},{8,9},{9,10},{10,11},{12,13},{... | collective-permute-start | bytes 147464 | tf_op jit(solution)/shard_map/ppermute | solution.py:25
  253.5 6.0 %collective-permute-start.3 = (f32[12,2,512]{2,1,0:T(2,128)S(1)}, f32[12,2,512]{2,1,0:T(2,128)S(1)}, u32[]{:S(2)}, u32[]{:S(2)}) collective-permute-start(f32[12,2,512]{2,1,0:T(2,128)S(1)} %get-tuple-element.268), channel_id=1, source_target_pairs={{1,0},{2,1},{3,2},{5,4},{6,5},{7,6},{9,8},{10,9},{11,10},{13,12},{... | collective-permute-start | bytes 147464 | tf_op jit(solution)/shard_map/ppermute | solution.py:27
  274.4 24.6 %copy-start = (f32[8,32,512]{2,1,0:T(8,128)}, f32[8,32,512]{2,1,0:T(8,128)S(1)}, u32[]{:S(2)}) copy-start(f32[8,32,512]{2,1,0:T(8,128)S(1)} %convolution_add_fusion.1) | copy-start | bytes 1572868
  274.4 7.2 %collective-permute-start.22 = (f32[2,32,512]{2,1,0:T(8,128)S(1)}, f32[2,32,512]{2,1,0:T(8,128)S(1)}, u32[]{:S(2)}, u32[]{:S(2)}) collective-permute-start(f32[2,32,512]{2,1,0:T(8,128)S(1)} %get-tuple-element.270), channel_id=1, source_target_pairs={{4,0},{8,4},{12,8},{16,12},{20,16},{24,20},{28,24},{32,28},{36,32}... | collective-permute-start | bytes 393224 | tf_op jit(solution)/shard_map/ppermute | solution.py:27
  279.1 9.6 %collective-permute-start.23 = (f32[2,32,512]{2,1,0:T(8,128)S(1)}, f32[2,32,512]{2,1,0:T(8,128)S(1)}, u32[]{:S(2)}, u32[]{:S(2)}) collective-permute-start(f32[2,32,512]{2,1,0:T(8,128)S(1)} %get-tuple-element.269), channel_id=1, source_target_pairs={{0,4},{4,8},{8,12},{12,16},{16,20},{20,24},{24,28},{28,32},{32,36}... | collective-permute-start | bytes 393224 | tf_op jit(solution)/shard_map/ppermute | solution.py:25
  288.7 6.2 %collective-permute-start.24 = (f32[12,2,512]{2,1,0:T(2,128)S(1)}, f32[12,2,512]{2,1,0:T(2,128)S(1)}, u32[]{:S(2)}, u32[]{:S(2)}) collective-permute-start(f32[12,2,512]{2,1,0:T(2,128)S(1)} %get-tuple-element.264), channel_id=1, source_target_pairs={{1,0},{2,1},{3,2},{5,4},{6,5},{7,6},{9,8},{10,9},{11,10},{13,12},{... | collective-permute-start | bytes 147464 | tf_op jit(solution)/shard_map/ppermute | solution.py:27
  292.3 6.0 %collective-permute-start.25 = (f32[12,2,512]{2,1,0:T(2,128)S(1)}, f32[12,2,512]{2,1,0:T(2,128)S(1)}, u32[]{:S(2)}, u32[]{:S(2)}) collective-permute-start(f32[12,2,512]{2,1,0:T(2,128)S(1)} %get-tuple-element.263), channel_id=1, source_target_pairs={{0,1},{1,2},{2,3},{4,5},{5,6},{6,7},{8,9},{9,10},{10,11},{12,13},{... | collective-permute-start | bytes 147464 | tf_op jit(solution)/shard_map/ppermute | solution.py:25
where the time goes:
time: 348 us; the launch traced here: 341 us
  starting transfers between devices  81.3 us (23%)
  matrix products  72.5 us (21%)
  blocking collectives  66.2 us (19%)
  other arithmetic  48.5 us (14%)
  local copies, waits for them, and re-layouts  45.4 us (13%)
  waiting for transfers between devices  24.2 us (7%)
    all_gather x1, blocking collectives, body(): gathered = lax.all_gather(packed, ('slab', 'pencil'), axis=0, tiled=True)  66.2 us
    ppermute x12, starting transfers between devices, extended(): lax.ppermute(head, axis, [((i + 1) % count, i) for i in range(ends)])  52.7 us
    another operation x1, local copies, waits for them, and re-layouts, restrict(): grid.reshape(planes // 2, 2, rows // 2, 2, length // 2, 2)  34.9 us
    ppermute x12, starting transfers between devices, extended(): lax.ppermute(tail, axis, [(i, (i + 1) % count) for i in range(ends)])  28.4 us
    dot_general x16, matrix products, pick(): jnp.einsum('ar,drx->adx', row_table, gradients, precision=lax.Precision.H...  27.9 us
    dot_general x16, matrix products, deposit(): added = jnp.dot(row_table.T, column_table, precision=lax.Precision.HIGHEST)  17.4 us
    add x3, other arithmetic, short_field(): accumulated + weight_of(step_z, step_y, step_x) * padded[corner_z:corner_...  16.9 us
    reduce_sum x4, other arithmetic, restrict(): grid.reshape(planes // 2, 2, rows // 2, 2, length // 2, 2)  14.4 us
  transfers between devices with their start and end apart: 26, of which 9 were waited for; matrix products, arithmetic and copies ran while one was open for 10% of the time, Pallas kernels for 0%

commit v1 on v0

v1 whole, which is shorter than its diff:
```python
import math

import jax
import jax.numpy as jnp
import numpy as np
from jax import lax
from jax.experimental import pallas as pl
from jax.experimental.pallas import tpu as pltpu
from jax.sharding import PartitionSpec as P

CZ = 8
CY = 32
NX = 512
NZ = 512
NY = 128
SLABS = 64
PENCILS = 4
ATOMS_DEV = 8192
F = 32
BF = jnp.bfloat16
F32 = jnp.float32
BOTH = ("slab", "pencil")
ROWS_V = 384
BLOCK_A = 1024
BLOCK_B = 512


def near_weight(squared):
    return 1.0 / math.sqrt(squared + 0.25) - 1.0 / math.sqrt(squared + 4.0)


def level_weight(level):
    return lambda squared: 2.0**-level * (1.0 / math.sqrt(squared + 1.0) - 1.0 / math.sqrt(squared + 4.0))


def interp_table(fine_ids, count, factor):
    fine_ids = np.asarray(fine_ids)
    numerator = np.clip(2 * fine_ids + 1 - factor, 0, 2 * factor * (count - 1))
    lower = np.minimum(numerator // (2 * factor), count - 2)
    fraction = (numerator - lower * 2 * factor) / (2.0 * factor)
    table = np.zeros((len(fine_ids), count))
    rows = np.arange(len(fine_ids))
    table[rows, lower] += 1.0 - fraction
    table[rows, lower + 1] += fraction
    return table


def split(table):
    high = np.asarray(table, np.float32).astype(BF)
    low = (np.asarray(table, np.float64) - high.astype(np.float64)).astype(BF)
    return np.concatenate([high, low], 0)


def window_table(weight, out_rows, out_start, valid, in_rows, in_start, height):
    table = np.zeros((height, 5 * in_rows))
    for c in range(3):
        for o in range(out_rows):
            y = out_start + o
            if not valid[0] <= y <= valid[1]:
                continue
            for a in range(-2, 3):
                for b in range(-2, 3):
                    i = y + b - in_start
                    table[c * out_rows + o, (a + 2) * in_rows + i] = weight(a * a + b * b + c * c)
    return split(table)


def coarse3_table():
    table = np.zeros((6 * 48, 64))
    weight = level_weight(3)
    for c in range(3):
        for o in range(3):
            for y in range(16):
                for k in range(7):
                    a = k - 3 - (o - 1)
                    for src in range(16):
                        b = src - y
                        if abs(a) > 2 or abs(b) > 2:
                            continue
                        r, j, i = src // 4, src // 2 % 2, src % 2
                        table[(c * 2 + j) * 48 + o * 16 + y, k * 8 + r * 2 + i] = weight(a * a + b * b + c * c)
    return split(table)


def coarse4_table():
    table = np.zeros((6 * 24, 64))
    weight = level_weight(4)
    for c in range(3):
        for o in range(3):
            for y in range(8):
                for k in range(7):
                    a = k - 3 - (o - 1)
                    for src in range(16):
                        b = src // 2 - y
                        if abs(a) > 2 or abs(b) > 2:
                            continue
                        r, j, i = src // 4, src // 2 % 2, src % 2
                        table[(c * 2 + j) * 24 + o * 8 + y, k * 8 + r * 2 + i] = weight(a * a + b * b + c * c)
    return split(table)


def spread(level):
    count = NX >> level
    to_fine = interp_table(np.arange(NX), count, 2**level).T
    cells = np.arange(count)
    blocks = []
    for c in range(3):
        near = (np.abs(cells[:, None] - cells[None, :]) == c).astype(np.float64)
        blocks.append(near @ to_fine)
    return blocks


def spread_halves(level):
    out = []
    x3 = np.arange(128) % 64
    for block in spread(level):
        for j in range(2):
            keep = (np.arange(128) // 64 == j)[:, None]
            out.append(np.where(keep, block[x3 >> (level - 3)], 0.0))
    return np.concatenate(out, 0)


def constants():
    out = {}
    sums = np.zeros((NX, NX))
    x = np.arange(NX)
    sums[x, x // 2] = 1.0
    sums[x, 256 + x // 4] = 1.0
    sums[x, 384 + x // 8] = 1.0
    sums[x, 448 + x // 8] = 1.0
    out["sums"] = sums.astype(BF)
    blocks = np.zeros((96, CZ * CY))
    row = np.arange(CZ * CY)
    blocks[row // 64 * 16 + row % 32 // 2, row] = 1.0
    blocks[64 + row // 128 * 8 + row % 32 // 4, row] = 1.0
    blocks[80 + row % 32 // 8, row] = 1.0
    out["block_sums"] = blocks.astype(BF)
    out["w0"] = window_table(near_weight, 40, -4, (-2, 33), 48, -8, 128)
    out["w1"] = window_table(level_weight(1), 24, -4, (-2, 17), 32, -8, 80)
    out["w2"] = window_table(level_weight(2), 16, -4, (-1, 8), 32, -8, 48)
    out["w3"] = coarse3_table()
    out["w4"] = coarse4_table()
    out["d1"] = np.concatenate(spread(1), 0).astype(BF)
    out["d2"] = np.concatenate(spread(2), 0).astype(BF)
    out["d3"] = spread_halves(3).astype(BF)
    out["d4"] = spread_halves(4).astype(BF)
    top = np.zeros((16, 128, 128))
    source = np.arange(128) % 64 // 4
    for c in range(16):
        top[c, :, :16] = np.abs(source[:, None] - np.arange(16)[None, :]) == c
    out["b5"] = top.reshape(2048, 128).astype(BF)
    fine5 = np.zeros((128, NX))
    fine5[:16] = interp_table(np.arange(NX), 16, F).T
    out["x5"] = fine5.astype(BF)
    along_z = np.zeros((SLABS, 16, ROWS_V))
    along_y = np.zeros((PENCILS, 40, ROWS_V))
    first = 0
    for level, planes, rows in ((1, 8, 24), (2, 4, 16), (3, 3, 16), (4, 3, 8), (5, 3, 4)):
        factor = 2**level
        table_z = interp_table(np.arange(NZ), NZ // factor, factor)
        table_y = interp_table(np.arange(NY), NY // factor, factor)
        for s in range(SLABS):
            base = (4 * s - 2, 2 * s - 1, s - 1, s // 2 - 1, int(np.clip((16 * s - 35) // 64, 0, 13)))[level - 1]
            for z in range(12):
                fine = CZ * s - 2 + z
                if not 0 <= fine < NZ:
                    continue
                for o in range(planes):
                    if 0 <= base + o < NZ // factor:
                        along_z[s, z, first + o * rows : first + (o + 1) * rows] = table_z[fine, base + o]
        for r in range(PENCILS):
            base = (16 * r - 4, 8 * r - 4, 0, 0, 0)[level - 1]
            for y in range(40):
                fine = CY * r - 4 + y
                if not 0 <= fine < NY:
                    continue
                for o in range(rows):
                    if 0 <= base + o < NY // factor:
                        along_y[r, y, first + o : first + planes * rows : rows] = table_y[fine, base + o]
        first += planes * rows
    out["uz"] = along_z.reshape(SLABS * 16, ROWS_V).astype(np.float32)
    out["uy"] = along_y.reshape(PENCILS * 40, ROWS_V).astype(np.float32)
    return out


def pieces(value):
    high = value.astype(BF)
    return high, (value - high.astype(F32)).astype(BF)


def dot(a, b):
    return jnp.dot(a, b, preferred_element_type=F32)


def weighted(table_ref, height, high, low):
    both = dot(table_ref[...], high)
    return both[:height] + both[height:] + dot(table_ref[0:height, :], low)


def times_exact(value, exact):
    high, low = pieces(value)
    rows = value.shape[0]
    both = dot(jnp.concatenate([high, low], 0), exact)
    return both[:rows] + both[rows:]


def shifted(value, step):
    lane = lax.broadcasted_iota(jnp.int32, value.shape, 1)
    rolled = pltpu.roll(value, (-step) % NX, 1)
    return jnp.where((lane + step >= 0) & (lane + step < NX), rolled, 0.0)


def deposit_kernel(pos, cell, charge, block_sums, sums, up, down, far_up, far_down, copies, acc):
    slab = pos[0]
    pencil = pos[1]
    acc[...] = jnp.zeros(acc.shape, F32)

    def step(block, carry):
        at = pl.ds(pl.multiple_of(block * BLOCK_A, BLOCK_A), BLOCK_A)
        row = (cell[0:1, at] - slab * CZ) * CY + (cell[1:2, at] - pencil * CY)
        column = cell[2:3, at]
        high = charge[0:1, at].astype(BF).astype(F32)
        low = charge[0:1, at] - high
        here = lax.broadcasted_iota(jnp.int32, (CZ * CY, BLOCK_A), 0) == row
        left = jnp.concatenate([jnp.where(here, high, 0.0).astype(BF), jnp.where(here, low, 0.0).astype(BF)], 0)
        right = jnp.where(lax.broadcasted_iota(jnp.int32, (NX, BLOCK_A), 0) == column, 1.0, 0.0).astype(BF)
        acc[...] += lax.dot_general(left, right, (((1,), (1,)), ((), ())), preferred_element_type=F32)
        return carry

    lax.fori_loop(0, ATOMS_DEV // BLOCK_A, step, 0)
    down[0:128, :] = acc[0:128, :] + acc[256:384, :]
    up[0:128, :] = acc[128:256, :] + acc[384:512, :]
    high_down, low_down = pieces(down[0:128, :])
    high_up, low_up = pieces(up[0:128, :])
    stack = dot(block_sums[:, 0:128], high_down) + dot(block_sums[:, 128:256], high_up)
    stack = stack + dot(block_sums[:, 0:128], low_down) + dot(block_sums[:, 128:256], low_up)
    coarse = times_exact(stack, sums[...])
    for ref in (down, up):
        ref[128:160, 0:256] = coarse[0:32, 0:256]
        ref[128:160, 256:512] = coarse[32:64, 0:256]
        ref[160:168, 0:128] = coarse[64:72, 256:384]
        ref[160:168, 128:256] = coarse[72:80, 256:384]
        ref[160:168, 256:512] = jnp.zeros((8, 256), F32)
    far_down[...] = coarse[64:72, 256:384]
    far_up[...] = coarse[72:80, 256:384]
    lane = lax.broadcasted_iota(jnp.int32, (2, 128), 1)
    mine = jnp.where(lane < 64, coarse[80:82, 384:512], coarse[82:84, 384:512])
    copies[...] = jnp.broadcast_to(mine[None], copies.shape)


def planes_of(pos, down, up, below, above, far_below, far_above):
    slab = pos[0]
    has_below = jnp.where(slab > 0, 1.0, 0.0)
    has_above = jnp.where(slab < SLABS - 1, 1.0, 0.0)
    has_far_below = jnp.where(slab > 1, 1.0, 0.0)
    has_far_above = jnp.where(slab < SLABS - 2, 1.0, 0.0)
    sources = ((below, has_below), (down, None), (up, None), (above, has_above))

    def masked(value, scale):
        return value if scale is None else value * scale

    def fine(k, first, count):
        ref, scale = sources[k // 4]
        at = k % 4 * 32 + first
        return masked(ref[at : at + count, :], scale)

    def level1(k, first, count):
        ref, scale = (sources[0], sources[1], sources[3])[k // 4]
        at = 128 + k % 2 * 16 + first
        lane = k % 4 // 2 * 256
        return masked(ref[at : at + count, lane : lane + 256], scale)

    def level2(k):
        if k == 0:
            return far_below[...] * has_far_below
        if k == 7:
            return far_above[...] * has_far_above
        ref, scale = (sources[0], sources[1], sources[3])[(k - 1) // 2]
        lane = (k - 1) % 2 * 128
        return masked(ref[160:168, lane : lane + 128], scale)

    return fine, level1, level2


def pack_kernel(pos, down, up, below, above, far_below, far_above, to_right, to_left):
    fine, level1, level2 = planes_of(pos, down, up, below, above, far_below, far_above)

    def packed(first, second, upper):
        sub = lax.broadcasted_iota(jnp.int32, first.shape, 0)
        other = pltpu.roll(second, 4, 0)
        return jnp.where(sub >= 4, first, other) if upper else jnp.where(sub < 4, first, other)

    for t in range(8):
        to_right[t * 8 : t * 8 + 8, :] = packed(fine(2 * t, 24, 8), fine(2 * t + 1, 24, 8), True)
        to_left[t * 8 : t * 8 + 8, :] = packed(fine(2 * t, 0, 8), fine(2 * t + 1, 0, 8), False)
    for t in range(6):
        rows = slice(64 + t // 2 * 8, 72 + t // 2 * 8)
        lanes = slice(t % 2 * 256, t % 2 * 256 + 256)
        to_right[rows, lanes] = packed(level1(2 * t, 8, 8), level1(2 * t + 1, 8, 8), True)
        to_left[rows, lanes] = packed(level1(2 * t, 0, 8), level1(2 * t + 1, 0, 8), False)
    for t in range(4):
        lanes = slice(t * 128, t * 128 + 128)
        to_right[88:96, lanes] = packed(level2(2 * t), level2(2 * t + 1), True)
        to_left[88:96, lanes] = packed(level2(2 * t), level2(2 * t + 1), False)


def coarse_fields(pos, level3, w3, w4, d3, d4, b5, x5, fields):
    slab = pos[0]

    def slab_rows(index):
        inside = jnp.where((index >= 0) & (index < SLABS), 1.0, 0.0)
        at = pl.multiple_of(jnp.clip(index, 0, SLABS - 1) * 8, 8)
        return level3[pl.ds(at, 8), :] * inside

    blank = jnp.zeros((8, 128), F32)
    near3 = jnp.concatenate([slab_rows(slab - 3 + k) for k in range(7)] + [blank], 0)
    parts = weighted(w3, 288, *pieces(near3))
    wide = jnp.concatenate([parts[k * 48 : k * 48 + 48] for k in range(6)], 1)
    fields[256:304, :] = times_exact(wide, d3[...])
    middle = 2 * (slab // 2)
    near4 = jnp.concatenate([slab_rows(middle - 6 + 2 * k) + slab_rows(middle - 5 + 2 * k) for k in range(7)] + [blank], 0)
    parts = weighted(w4, 144, *pieces(near4))
    wide = jnp.concatenate([parts[k * 24 : k * 24 + 24] for k in range(6)] , 1)
    wide = jnp.concatenate([wide, jnp.zeros((8, 768), F32)], 0)
    fields[304:328, :] = times_exact(wide, d4[...])[0:24]
    every = level3[...].reshape(16, 4, 8, 128)
    tops = jnp.sum(every, axis=1).reshape(128, 128)
    row = lax.broadcasted_iota(jnp.int32, (256, 128), 0)
    source = lax.broadcasted_iota(jnp.int32, (256, 128), 1)
    first_plane = jnp.clip(jnp.right_shift(16 * slab - 35, 6), 0, 13)
    step_x = (row // 16).astype(F32)
    step_z = (first_plane + row % 16 // 4 - source // 8).astype(F32)
    step_y = (row % 4 - source % 8 // 2).astype(F32)
    kernel = (1.0 / F) / jnp.sqrt(step_z * step_z + step_y * step_y + step_x * step_x + 1.0)
    kernel_high, kernel_low = pieces(kernel)
    top_high, top_low = pieces(tops)
    parts = dot(kernel_high, top_high) + dot(kernel_low, top_high) + dot(kernel_high, top_low)
    wide = jnp.concatenate([parts[k * 16 : k * 16 + 16] for k in range(16)], 1)
    fields[328:344, :] = times_exact(times_exact(wide, b5[...]), x5[...])
    fields[344:384, :] = jnp.zeros((40, NX), F32)


def field_kernel(
    pos, cell, charge, down, up, below, above, far_below, far_above, left, right, level3,
    uz, uy, w0, w1, w2, w3, w4, d1, d2, d3, d4, b5, x5,
    potential, forces,
    high0, low0, high1, low1, high2, low2, fields, weights, wide1, wide2, grid, slopes,
):
    slab = pos[0]
    pencil = pos[1]
    has_left = jnp.where(pencil > 0, 1.0, 0.0)
    has_right = jnp.where(pencil < PENCILS - 1, 1.0, 0.0)
    fine, level1, level2 = planes_of(pos, down, up, below, above, far_below, far_above)

    def halo(ref, scale, k, rows, lanes):
        tile = ref[rows, lanes] * scale
        return tile if k % 2 == 0 else pltpu.roll(tile, 4, 0)

    every = slice(0, NX)
    for k in range(16):
        rows = slice(k // 2 * 8, k // 2 * 8 + 8)
        plane = jnp.concatenate(
            [halo(left, has_left, k, rows, every), fine(k, 0, 32), halo(right, has_right, k, rows, every)], 0
        )
        high0[k * 48 : k * 48 + 48, :], low0[k * 48 : k * 48 + 48, :] = pieces(plane)
    for k in range(12):
        t = k // 2
        rows = slice(64 + t // 2 * 8, 72 + t // 2 * 8)
        lanes = slice(t % 2 * 256, t % 2 * 256 + 256)
        plane = jnp.concatenate(
            [halo(left, has_left, k, rows, lanes), level1(k, 0, 16), halo(right, has_right, k, rows, lanes)], 0
        )
        high1[k * 32 : k * 32 + 32, :], low1[k * 32 : k * 32 + 32, :] = pieces(plane)
    for k in range(8):
        lanes = slice(k // 2 * 128, k // 2 * 128 + 128)
        plane = jnp.concatenate(
            [
                halo(left, has_left, k, slice(88, 96), lanes),
                level2(k),
                halo(right, has_right, k, slice(88, 96), lanes),
                jnp.zeros((8, 128), F32),
            ],
            0,
        )
        high2[k * 32 : k * 32 + 32, :], low2[k * 32 : k * 32 + 32, :] = pieces(plane)

    coarse_fields(pos, level3, w3, w4, d3, d4, b5, x5, fields)
    for o in range(8):
        parts = weighted(w1, 80, high1[o * 32 : o * 32 + 160, :], low1[o * 32 : o * 32 + 160, :])
        for c in range(3):
            wide1[o * 24 : o * 24 + 24, c * 256 : c * 256 + 256] = parts[c * 24 : c * 24 + 24]
    fields[0:192, :] = times_exact(wide1[...], d1[...])
    for o in range(4):
        parts = weighted(w2, 48, high2[o * 32 : o * 32 + 160, :], low2[o * 32 : o * 32 + 160, :])
        for c in range(3):
            wide2[o * 16 : o * 16 + 16, c * 128 : c * 128 + 128] = parts[c * 16 : c * 16 + 16]
    fields[192:256, :] = times_exact(wide2[...], d2[...])

    for z in range(12):
        weights[z * 40 : z * 40 + 40, :] = uy[...] * uz[z : z + 1, :]
    weight_high, weight_low = pieces(weights[...])
    field_high, field_low = pieces(fields[...])
    grid[...] = dot(weight_high, field_high) + dot(weight_low, field_high) + dot(weight_high, field_low)
    line = lax.broadcasted_iota(jnp.int32, (40, NX), 0)
    inside = jnp.where(line < 4, has_left, jnp.where(line >= 36, has_right, 1.0))
    for z in range(12):
        parts = weighted(w0, 128, high0[z * 48 : z * 48 + 240, :], low0[z * 48 : z * 48 + 240, :])
        near, one, two = parts[0:40], parts[40:80], parts[80:120]
        near = near + (shifted(one, 1) + shifted(one, -1)) + (shifted(two, 2) + shifted(two, -2))
        value = (grid[z * 40 : z * 40 + 40, :] + near) * inside
        if z < 2:
            value = value * jnp.where(slab > 0, 1.0, 0.0)
        if z >= 10:
            value = value * jnp.where(slab < SLABS - 1, 1.0, 0.0)
        grid[z * 40 : z * 40 + 40, :] = value

    def slope(ahead, behind, far_ahead, far_behind):
        return (8.0 * (ahead - behind) - (far_ahead - far_behind)) * (1.0 / 12.0)

    for z in range(8):
        at = (z + 2) * 40 + 4

        def part(step_z, step_y):
            start = at + step_z * 40 + step_y
            return grid[start : start + 32, :]

        own = part(0, 0)
        potential[z * 32 : z * 32 + 32, :] = own
        along = (
            slope(part(1, 0), part(-1, 0), part(2, 0), part(-2, 0)),
            slope(part(0, 1), part(0, -1), part(0, 2), part(0, -2)),
            slope(shifted(own, 1), shifted(own, -1), shifted(own, 2), shifted(own, -2)),
        )
        for d in range(3):
            rows = slice(d * 256 + z * 32, d * 256 + z * 32 + 32)
            slopes[rows, 0:512], slopes[rows, 512:1024] = pieces(along[d])

    def step(block, carry):
        at = pl.ds(pl.multiple_of(block * BLOCK_B, BLOCK_B), BLOCK_B)
        row = (cell[0:1, at] - slab * CZ) * CY + (cell[1:2, at] - pencil * CY)
        column = cell[2:3, at]
        chosen = jnp.where(lax.broadcasted_iota(jnp.int32, (NX, BLOCK_B), 0) == column, 1.0, 0.0).astype(BF)
        lines = dot(slopes[...], jnp.concatenate([chosen, chosen], 0))
        here = lax.broadcasted_iota(jnp.int32, (CZ * CY, BLOCK_B), 0) == row
        for d in range(3):
            picked = jnp.sum(jnp.where(here, lines[d * 256 : d * 256 + 256], 0.0), axis=0, keepdims=True)
            forces[d : d + 1, at] = -charge[0:1, at] * picked
        return carry

    lax.fori_loop(0, ATOMS_DEV // BLOCK_B, step, 0)


def whole(count):
    return [pl.BlockSpec(memory_space=pltpu.SMEM)] + [pl.BlockSpec(memory_space=pltpu.VMEM)] * count


def rotated(value, slab_step, pencil_step):
    pairs = [
        (s * PENCILS + r, (s + slab_step) % SLABS * PENCILS + (r + pencil_step) % PENCILS)
        for s in range(SLABS)
        for r in range(PENCILS)
    ]
    return lax.ppermute(value, BOTH, pairs)


def f32_shape(*shape):
    return jax.ShapeDtypeStruct(shape, F32)


def make_body(tables):
    params = pltpu.CompilerParams(vmem_limit_bytes=48 * 2**20)

    def body(atom_cell, charge):
        slab = lax.axis_index("slab")
        pencil = lax.axis_index("pencil")
        pos = jnp.stack([slab, pencil]).astype(jnp.int32)
        charge = charge.reshape(1, ATOMS_DEV)
        up, down, far_up, far_down, copies = pl.pallas_call(
            deposit_kernel,
            out_shape=(f32_shape(168, NX), f32_shape(168, NX), f32_shape(8, 128), f32_shape(8, 128), f32_shape(256, 2, 128)),
            in_specs=whole(4),
            out_specs=[pl.BlockSpec(memory_space=pltpu.VMEM)] * 5,
            scratch_shapes=[pltpu.VMEM((512, NX), F32)],
            compiler_params=params,
            name="deposit",
        )(pos, atom_cell, charge, jnp.asarray(tables["block_sums"]), jnp.asarray(tables["sums"]))
        below = rotated(up, 1, 0)
        above = rotated(down, -1, 0)
        far_below = rotated(far_up, 2, 0)
        far_above = rotated(far_down, -2, 0)
        level3 = lax.all_to_all(copies, BOTH, 0, 0, tiled=True).reshape(512, 128)
        to_right, to_left = pl.pallas_call(
            pack_kernel,
            out_shape=(f32_shape(96, NX), f32_shape(96, NX)),
            in_specs=whole(6),
            out_specs=[pl.BlockSpec(memory_space=pltpu.VMEM)] * 2,
            compiler_params=params,
            name="pack",
        )(pos, down, up, below, above, far_below, far_above)
        left = rotated(to_right, 0, 1)
        right = rotated(to_left, 0, -1)
        uz = lax.dynamic_slice_in_dim(jnp.asarray(tables["uz"]), slab * 16, 16, 0)
        uy = lax.dynamic_slice_in_dim(jnp.asarray(tables["uy"]), pencil * 40, 40, 0)
        names = ("w0", "w1", "w2", "w3", "w4", "d1", "d2", "d3", "d4", "b5", "x5")
        potential, forces = pl.pallas_call(
            field_kernel,
            out_shape=(f32_shape(CZ * CY, NX), f32_shape(3, ATOMS_DEV)),
            in_specs=whole(13 + len(names)),
            out_specs=[pl.BlockSpec(memory_space=pltpu.VMEM)] * 2,
            scratch_shapes=[
                pltpu.VMEM((768, NX), BF),
                pltpu.VMEM((768, NX), BF),
                pltpu.VMEM((384, 256), BF),
                pltpu.VMEM((384, 256), BF),
                pltpu.VMEM((256, 128), BF),
                pltpu.VMEM((256, 128), BF),
                pltpu.VMEM((ROWS_V, NX), F32),
                pltpu.VMEM((480, ROWS_V), F32),
                pltpu.VMEM((192, 768), F32),
                pltpu.VMEM((64, 384), F32),
                pltpu.VMEM((480, NX), F32),
                pltpu.VMEM((768, 1024), BF),
            ],
            compiler_params=params,
            name="field",
        )(
            pos, atom_cell, charge, down, up, below, above, far_below, far_above, left, right, level3,
            uz, uy, *[jnp.asarray(tables[name]) for name in names],
        )
        return (potential.reshape(CZ, CY, NX), forces)

    return body


def solution(mesh):
    return jax.shard_map(
        make_body(constants()),
        mesh=mesh,
        in_specs=(P(None, BOTH), P(BOTH)),
        out_specs=(P("slab", "pencil", None), P(None, BOTH)),
        check_vma=False,
    )
```

time: 348 us -> 86 us (0.25)
  the two profiles are of different devices: /device:TPU:136 before, /device:TPU:24 now
where the time goes in v1:
time: 86 us; the launch traced here: 85 us
  Pallas kernels  33 us (38%)
  starting transfers between devices  26.4 us (31%)
  local copies, waits for them, and re-layouts  16.8 us (20%)
  waiting for transfers between devices  8 us (9%)
    pallas_call x1, Pallas kernels, body(): pl.pallas_call(field_kernel, out_shape=(f32_shape(CZ * CY, NX), f32_shape...  24.5 us
    ppermute x6, starting transfers between devices, rotated(): return lax.ppermute(value, BOTH, pairs)  16.4 us
    unnamed x46, local copies, waits for them, and re-layouts  14.6 us
    all_to_all x1, starting transfers between devices, body(): level3 = lax.all_to_all(copies, BOTH, 0, 0, tiled=True).reshape(512, 128)  9.96 us
    ppermute x6, waiting for transfers between devices, rotated(): return lax.ppermute(value, BOTH, pairs)  7.99 us
    pallas_call x1, Pallas kernels, body(): pl.pallas_call(deposit_kernel, out_shape=(f32_shape(168, NX), f32_shape(1...  7.16 us
  transfers between devices with their start and end apart: 7, of which 3 were waited for; matrix products, arithmetic and copies ran while one was open for 3% of the time, Pallas kernels for 2%

profile of v1, /device:TPU:24, one launch (start us, length us, event | category | flops | bytes accessed | tf_op | source)
XLA Modules:
  0.0 85.0 jit_solution(4345317080951166449)
XLA Ops:
  0.6 0.0 copy-start
  0.6 0.0 copy-start.1
  0.7 0.1 pad_add_fusion.pos
  0.7 0.0 copy-start.21
  0.7 0.0 copy-start.3
  0.7 1.0 %copy-done.3 = s32[3,8192]{1,0:T(4,128)S(1)} copy-done((s32[3,8192]{1,0:T(4,128)S(1)}, s32[3,8192]{1,0:T(4,128)}, u32[]{:S(2)}) %copy-start.3) | copy-done | bytes 98328
  1.7 0.0 copy-start.5
  1.7 1.0 %copy-done.5 = bf16[512,512]{1,0:T(8,128)(2,1)S(1)} copy-done((bf16[512,512]{1,0:T(8,128)(2,1)S(1)}, bf16[512,512]{1,0:T(8,128)(2,1)}, u32[]{:S(2)}) %copy-start.5) | copy-done | bytes 524312
  2.8 0.0 copy-start.10
  2.8 0.8 copy-done.10
  3.5 0.0 copy-start.18
  3.5 0.8 copy-done.18
  4.3 0.0 copy-start.4
  4.3 0.0 copy-start.9
  4.3 7.2 %deposit.1 = (f32[168,512]{1,0:T(8,128)S(1)}, f32[168,512]{1,0:T(8,128)S(1)}, f32[8,128]{1,0:T(8,128)S(1)}, f32[8,128]{1,0:T(8,128)S(1)}, f32[256,2,128]{2,1,0:T(2,128)S(1)}) custom-call(s32[2]{0:T(128)S(1)} %pad_add_fusion.pos, s32[3,8192]{1,0:T(4,128)S(1)} %copy-done.3, f32[1,8192]{1,0:T(1,128)S(1)} %bitcast.6, bf16[96,256]{1,0:T(8,128)(2,1)S(1)} %copy-done.18, ...), custom_call_target="tpu_custom_call" | custom-call | tf_op jit(solution)/shard_map/deposit/pallas_call | solution.py:478
  11.5 0.0 copy-start.8
  11.5 0.7 copy-done.8
  12.2 7.5 %collective-permute-start.1 = (f32[168,512]{1,0:T(8,128)S(1)}, f32[168,512]{1,0:T(8,128)S(1)}, u32[]{:S(2)}, u32[]{:S(2)}) collective-permute-start(f32[168,512]{1,0:T(8,128)S(1)} %get-tuple-element.11.down), channel_id=1, source_target_pairs={{0,252},{1,253},{2,254},{3,255},{4,0},{5,1},{6,2},{7,3},{8,4},{9,5... | collective-permute-start | bytes 1032200 | tf_op jit(solution)/shard_map/ppermute | solution.py:463
  19.7 0.0 collective-permute-start
  19.7 10.0 %all-to-all-start = ((f32[256,2,128]{2,1,0:T(2,128)}), f32[256,2,128]{2,1,0:T(2,128)S(1)}, u32[]{:S(2)}, u32[]{:S(2)}) async-start(f32[256,2,128]{2,1,0:T(2,128)} %copy-done.8), calls=%async_computation | async-start | bytes 524288 | tf_op jit(solution)/shard_map/all_to_all | solution.py:491
  29.7 1.6 %collective-permute-start.2 = (f32[8,128]{1,0:T(8,128)S(1)}, f32[8,128]{1,0:T(8,128)S(1)}, u32[]{:S(2)}, u32[]{:S(2)}) collective-permute-start(f32[8,128]{1,0:T(8,128)S(1)} %get-tuple-element.13), channel_id=1, source_target_pairs={{0,8},{1,9},{2,10},{3,11},{4,12},{5,13},{6,14},{7,15},{8,16},{9,17... | collective-permute-start | bytes 12296 | tf_op jit(solution)/shard_map/ppermute | solution.py:463
  31.2 5.3 %collective-permute-start.3 = (f32[8,128]{1,0:T(8,128)S(1)}, f32[8,128]{1,0:T(8,128)S(1)}, u32[]{:S(2)}, u32[]{:S(2)}) collective-permute-start(f32[8,128]{1,0:T(8,128)S(1)} %get-tuple-element.14), channel_id=1, source_target_pairs={{0,248},{1,249},{2,250},{3,251},{4,252},{5,253},{6,254},{7,255},{8... | collective-permute-start | bytes 12296 | tf_op jit(solution)/shard_map/ppermute | solution.py:463
  36.6 4.4 %collective-permute-done.2.far_below = f32[8,128]{1,0:T(8,128)S(1)} collective-permute-done((f32[8,128]{1,0:T(8,128)S(1)}, f32[8,128]{1,0:T(8,128)S(1)}, u32[]{:S(2)}, u32[]{:S(2)}) %collective-permute-start.2) | collective-permute-done | bytes 4128 | tf_op jit(solution)/shard_map/ppermute | solution.py:463
  41.0 0.0 collective-permute-done.3.far_above
  41.0 0.0 copy-start.19
  41.0 0.0 collective-permute-done.1.above
  41.0 0.0 collective-permute-done.below
  41.0 1.4 %pack.1 = (f32[96,512]{1,0:T(8,128)}, f32[96,512]{1,0:T(8,128)}) custom-call(s32[2]{0:T(128)S(1)} %pad_add_fusion.pos, f32[168,512]{1,0:T(8,128)S(1)} %get-tuple-element.11.down, f32[168,512]{1,0:T(8,128)S(1)} %get-tuple-element.12.up, f32[168,512]{1,0:T(8,128)S(1)} %collective-permute-done.below, f32[168,512]{1,0:T(8,128)S(1)} %collective-permute-done.1.above, ...), custom_call_target="tpu_custom_call" | custom-call | tf_op jit(solution)/shard_map/pack/pallas_call | solution.py:492
  42.4 0.4 collective-permute-start.4
  42.7 1.7 %collective-permute-start.5 = (f32[96,512]{1,0:T(8,128)}, f32[96,512]{1,0:T(8,128)}, u32[]{:S(2)}, u32[]{:S(2)}) collective-permute-start(f32[96,512]{1,0:T(8,128)} %get-tuple-element.16), channel_id=1, source_target_pairs={{0,3},{1,0},{2,1},{3,2},{4,7},{5,4},{6,5},{7,6},{8,11},{9,8},{10,9... | collective-permute-start | bytes 589832 | tf_op jit(solution)/shard_map/ppermute | solution.py:463
  44.4 0.0 copy-done.21
  44.4 0.0 copy-done.19
  44.4 1.3 %constant_dynamic-slice_fusion.1.uz = f32[16,384]{1,0:T(8,128)} fusion(f32[1024,384]{1,0:T(8,128)} %constant.51.clone, s32[]{:T(128)S(6)} %select_n.6), kind=kLoop, calls=%fused_computation.2 | loop fusion | bytes 49156 | tf_op jit(solution)/shard_map/dynamic_slice | solution.py:502
  45.7 0.8 constant_dynamic-slice_fusion.uy
  46.6 0.0 all-to-all-done
  46.6 2.3 %collective-permute-done.4.left = f32[96,512]{1,0:T(8,128)} collective-permute-done((f32[96,512]{1,0:T(8,128)}, f32[96,512]{1,0:T(8,128)}, u32[]{:S(2)}, u32[]{:S(2)}) %collective-permute-start.4) | collective-permute-done | bytes 196640 | tf_op jit(solution)/shard_map/ppermute | solution.py:463
  48.8 1.3 %collective-permute-done.5.right = f32[96,512]{1,0:T(8,128)} collective-permute-done((f32[96,512]{1,0:T(8,128)}, f32[96,512]{1,0:T(8,128)}, u32[]{:S(2)}, u32[]{:S(2)}) %collective-permute-start.5) | collective-permute-done | bytes 196640 | tf_op jit(solution)/shard_map/ppermute | solution.py:463
  50.2 0.0 copy-done
  50.2 0.0 copy-done.1
  50.2 0.0 copy-done.4
  50.2 0.0 copy-done.9
  50.2 0.0 copy-start.2
  50.2 1.1 %copy-done.2 = bf16[768,512]{1,0:T(8,128)(2,1)S(1)} copy-done((bf16[768,512]{1,0:T(8,128)(2,1)S(1)}, bf16[768,512]{1,0:T(8,128)(2,1)}, u32[]{:S(2)}) %copy-start.2) | copy-done | bytes 786456
  51.3 0.0 copy-start.6
  51.3 1.0 %copy-done.6 = bf16[2048,128]{1,0:T(8,128)(2,1)S(1)} copy-done((bf16[2048,128]{1,0:T(8,128)(2,1)S(1)}, bf16[2048,128]{1,0:T(8,128)(2,1)}, u32[]{:S(2)}) %copy-start.6) | copy-done | bytes 524312
  52.4 0.0 copy-start.7
  52.4 1.0 %copy-done.7 = bf16[384,512]{1,0:T(8,128)(2,1)S(1)} copy-done((bf16[384,512]{1,0:T(8,128)(2,1)S(1)}, bf16[384,512]{1,0:T(8,128)(2,1)}, u32[]{:S(2)}) %copy-start.7) | copy-done | bytes 393240
  53.4 0.0 copy-start.11
  53.4 0.8 copy-done.11
  54.1 0.0 copy-start.12
  54.1 0.9 %copy-done.12 = bf16[128,512]{1,0:T(8,128)(2,1)S(1)} copy-done((bf16[128,512]{1,0:T(8,128)(2,1)S(1)}, bf16[128,512]{1,0:T(8,128)(2,1)}, u32[]{:S(2)}) %copy-start.12) | copy-done | bytes 131096
  55.0 0.0 copy-start.13
  55.0 0.9 %copy-done.13 = bf16[256,240]{1,0:T(8,128)(2,1)S(1)} copy-done((bf16[256,240]{1,0:T(8,128)(2,1)S(1)}, bf16[256,240]{1,0:T(8,128)(2,1)}, u32[]{:S(2)}) %copy-start.13) | copy-done | bytes 122904
  55.9 0.0 copy-start.14
  55.9 0.7 copy-done.14
  56.7 0.0 copy-start.15
  56.7 0.9 %copy-done.15 = bf16[160,160]{1,0:T(8,128)(2,1)S(1)} copy-done((bf16[160,160]{1,0:T(8,128)(2,1)S(1)}, bf16[160,160]{1,0:T(8,128)(2,1)}, u32[]{:S(2)}) %copy-start.15) | copy-done | bytes 51224
  57.5 0.0 copy-start.16
  57.5 0.9 %copy-done.16 = bf16[288,64]{1,0:T(8,128)(2,1)S(1)} copy-done((bf16[288,64]{1,0:T(8,128)(2,1)S(1)}, bf16[288,64]{1,0:T(8,128)(2,1)}, u32[]{:S(2)}) %copy-start.16) | copy-done | bytes 36888
  58.4 0.0 copy-start.17
  58.4 0.8 copy-done.17
  59.2 0.7 copy-done.20
  59.9 0.6 copy-done.22
  60.5 24.5 %field.1 = (f32[256,512]{1,0:T(8,128)}, f32[3,8192]{1,0:T(4,128)}) custom-call(s32[2]{0:T(128)S(1)} %copy-done.22, s32[3,8192]{1,0:T(4,128)S(1)} %copy-done.4, f32[1,8192]{1,0:T(1,128)S(1)} %bitcast.7, f32[168,512]{1,0:T(8,128)S(1)} %get-tuple-element.11.down, f32[168,512]{1,0:T(8,128)S(1)} %get-tuple-element.12.up, ...), custom_call_target="tpu_custom_call" | custom-call | tf_op jit(solution)/shard_map/field/pallas_call | solution.py:505
  (2 shorter events, 0.0 us)
Async XLA Ops:
  0.6 49.5 %copy-start = (bf16[768,512]{1,0:T(8,128)(2,1)S(1)}, bf16[768,512]{1,0:T(8,128)(2,1)}, u32[]{:S(2)}) copy-start(bf16[768,512]{1,0:T(8,128)(2,1)} %constant.61.clone.d4) | copy-start | bytes 2359300
  0.6 49.5 %copy-start.1 = (bf16[768,512]{1,0:T(8,128)(2,1)S(1)}, bf16[768,512]{1,0:T(8,128)(2,1)}, u32[]{:S(2)}) copy-start(bf16[768,512]{1,0:T(8,128)(2,1)} %constant.60.clone.d3) | copy-start | bytes 2359300
  0.7 43.7 %copy-start.21 = (s32[2]{0:T(128)}, s32[2]{0:T(128)S(1)}, u32[]{:S(2)}) copy-start(s32[2]{0:T(128)S(1)} %pad_add_fusion.pos) | copy-start | bytes 28
  0.7 1.0 %copy-start.3 = (s32[3,8192]{1,0:T(4,128)S(1)}, s32[3,8192]{1,0:T(4,128)}, u32[]{:S(2)}) copy-start(s32[3,8192]{1,0:T(4,128)} %cell.3) | copy-start | bytes 294916
  1.7 1.0 %copy-start.5 = (bf16[512,512]{1,0:T(8,128)(2,1)S(1)}, bf16[512,512]{1,0:T(8,128)(2,1)}, u32[]{:S(2)}) copy-start(bf16[512,512]{1,0:T(8,128)(2,1)} %constant.50.clone.sums) | copy-start | bytes 1572868
  2.8 0.8 copy-start.10
  3.5 0.8 copy-start.18
  4.3 45.8 %copy-start.4 = (s32[3,8192]{1,0:T(4,128)S(1)}, s32[3,8192]{1,0:T(4,128)}, u32[]{:S(2)}) copy-start(s32[3,8192]{1,0:T(4,128)} %cell.3) | copy-start | bytes 294916
  4.3 45.8 %copy-start.9 = (bf16[576,64]{1,0:T(8,128)(2,1)S(1)}, bf16[576,64]{1,0:T(8,128)(2,1)}, u32[]{:S(2)}) copy-start(bf16[576,64]{1,0:T(8,128)(2,1)} %constant.56.clone.w3) | copy-start | bytes 221188
  11.5 0.7 copy-start.8
  12.2 28.8 %collective-permute-start.1 = (f32[168,512]{1,0:T(8,128)S(1)}, f32[168,512]{1,0:T(8,128)S(1)}, u32[]{:S(2)}, u32[]{:S(2)}) collective-permute-start(f32[168,512]{1,0:T(8,128)S(1)} %get-tuple-element.11.down), channel_id=1, source_target_pairs={{0,252},{1,253},{2,254},{3,255},{4,0},{5,1},{6,2},{7,3},{8,4},{9,5... | collective-permute-start | bytes 1032200 | tf_op jit(solution)/shard_map/ppermute | solution.py:463
  19.7 21.3 %collective-permute-start = (f32[168,512]{1,0:T(8,128)S(1)}, f32[168,512]{1,0:T(8,128)S(1)}, u32[]{:S(2)}, u32[]{:S(2)}) collective-permute-start(f32[168,512]{1,0:T(8,128)S(1)} %get-tuple-element.12.up), channel_id=1, source_target_pairs={{0,4},{1,5},{2,6},{3,7},{4,8},{5,9},{6,10},{7,11},{8,12},{9,13},{1... | collective-permute-start | bytes 1032200 | tf_op jit(solution)/shard_map/ppermute | solution.py:463
  19.7 26.9 %all-to-all-start = ((f32[256,2,128]{2,1,0:T(2,128)}), f32[256,2,128]{2,1,0:T(2,128)S(1)}, u32[]{:S(2)}, u32[]{:S(2)}) async-start(f32[256,2,128]{2,1,0:T(2,128)} %copy-done.8), calls=%async_computation | async-start | bytes 524288 | tf_op jit(solution)/shard_map/all_to_all | solution.py:491
  29.7 11.3 %collective-permute-start.2 = (f32[8,128]{1,0:T(8,128)S(1)}, f32[8,128]{1,0:T(8,128)S(1)}, u32[]{:S(2)}, u32[]{:S(2)}) collective-permute-start(f32[8,128]{1,0:T(8,128)S(1)} %get-tuple-element.13), channel_id=1, source_target_pairs={{0,8},{1,9},{2,10},{3,11},{4,12},{5,13},{6,14},{7,15},{8,16},{9,17... | collective-permute-start | bytes 12296 | tf_op jit(solution)/shard_map/ppermute | solution.py:463
  31.2 9.7 %collective-permute-start.3 = (f32[8,128]{1,0:T(8,128)S(1)}, f32[8,128]{1,0:T(8,128)S(1)}, u32[]{:S(2)}, u32[]{:S(2)}) collective-permute-start(f32[8,128]{1,0:T(8,128)S(1)} %get-tuple-element.14), channel_id=1, source_target_pairs={{0,248},{1,249},{2,250},{3,251},{4,252},{5,253},{6,254},{7,255},{8... | collective-permute-start | bytes 12296 | tf_op jit(solution)/shard_map/ppermute | solution.py:463
  41.0 3.4 %copy-start.19 = (f32[8,128]{1,0:T(8,128)}, f32[8,128]{1,0:T(8,128)S(1)}, u32[]{:S(2)}) copy-start(f32[8,128]{1,0:T(8,128)S(1)} %collective-permute-done.3.far_above) | copy-start | bytes 12292
  42.4 6.5 %collective-permute-start.4 = (f32[96,512]{1,0:T(8,128)}, f32[96,512]{1,0:T(8,128)}, u32[]{:S(2)}, u32[]{:S(2)}) collective-permute-start(f32[96,512]{1,0:T(8,128)} %get-tuple-element.15), channel_id=1, source_target_pairs={{0,1},{1,2},{2,3},{3,0},{4,5},{5,6},{6,7},{7,4},{8,9},{9,10},{10,1... | collective-permute-start | bytes 589832 | tf_op jit(solution)/shard_map/ppermute | solution.py:463
  42.7 7.4 %collective-permute-start.5 = (f32[96,512]{1,0:T(8,128)}, f32[96,512]{1,0:T(8,128)}, u32[]{:S(2)}, u32[]{:S(2)}) collective-permute-start(f32[96,512]{1,0:T(8,128)} %get-tuple-element.16), channel_id=1, source_target_pairs={{0,3},{1,0},{2,1},{3,2},{4,7},{5,4},{6,5},{7,6},{8,11},{9,8},{10,9... | collective-permute-start | bytes 589832 | tf_op jit(solution)/shard_map/ppermute | solution.py:463
  50.2 1.1 %copy-start.2 = (bf16[768,512]{1,0:T(8,128)(2,1)S(1)}, bf16[768,512]{1,0:T(8,128)(2,1)}, u32[]{:S(2)}) copy-start(bf16[768,512]{1,0:T(8,128)(2,1)} %constant.58.clone.d1) | copy-start | bytes 2359300
  51.3 1.0 %copy-start.6 = (bf16[2048,128]{1,0:T(8,128)(2,1)S(1)}, bf16[2048,128]{1,0:T(8,128)(2,1)}, u32[]{:S(2)}) copy-start(bf16[2048,128]{1,0:T(8,128)(2,1)} %constant.62.clone.b5) | copy-start | bytes 1572868
  52.4 1.0 %copy-start.7 = (bf16[384,512]{1,0:T(8,128)(2,1)S(1)}, bf16[384,512]{1,0:T(8,128)(2,1)}, u32[]{:S(2)}) copy-start(bf16[384,512]{1,0:T(8,128)(2,1)} %constant.59.clone.d2) | copy-start | bytes 1179652
  53.4 0.8 copy-start.11
  54.1 0.9 %copy-start.12 = (bf16[128,512]{1,0:T(8,128)(2,1)S(1)}, bf16[128,512]{1,0:T(8,128)(2,1)}, u32[]{:S(2)}) copy-start(bf16[128,512]{1,0:T(8,128)(2,1)} %constant.63.clone.x5) | copy-start | bytes 393220
  55.0 0.9 %copy-start.13 = (bf16[256,240]{1,0:T(8,128)(2,1)S(1)}, bf16[256,240]{1,0:T(8,128)(2,1)}, u32[]{:S(2)}) copy-start(bf16[256,240]{1,0:T(8,128)(2,1)} %constant.53.clone.w0) | copy-start | bytes 368644
  55.9 0.7 copy-start.14
  56.7 0.9 %copy-start.15 = (bf16[160,160]{1,0:T(8,128)(2,1)S(1)}, bf16[160,160]{1,0:T(8,128)(2,1)}, u32[]{:S(2)}) copy-start(bf16[160,160]{1,0:T(8,128)(2,1)} %constant.54.clone.w1) | copy-start | bytes 153604
  57.5 0.9 %copy-start.16 = (bf16[288,64]{1,0:T(8,128)(2,1)S(1)}, bf16[288,64]{1,0:T(8,128)(2,1)}, u32[]{:S(2)}) copy-start(bf16[288,64]{1,0:T(8,128)(2,1)} %constant.57.clone.w4) | copy-start | bytes 110596
  58.4 0.8 copy-start.17
  59.2 0.7 copy-start.20
  59.9 0.6 copy-start.22

commit v2 on v1

--- a/solution.py
+++ b/solution.py
@@ -1,4 +1,5 @@
 import math
+from functools import partial
 
 import jax
 import jax.numpy as jnp
@@ -22,6 +23,7 @@
 BOTH = ("slab", "pencil")
 ROWS_V = 384
 BLOCK_A = 1024
+BANK_ROWS = 28672
 BLOCK_B = 512
 
 
@@ -148,7 +150,7 @@
     source = np.arange(128) % 64 // 4
     for c in range(16):
         top[c, :, :16] = np.abs(source[:, None] - np.arange(16)[None, :]) == c
-    out["b5"] = top.reshape(2048, 128).astype(BF)
+    out["b5"] = top.reshape(4, 512, 128).transpose(1, 0, 2).reshape(512, 512).astype(BF)
     fine5 = np.zeros((128, NX))
     fine5[:16] = interp_table(np.arange(NX), 16, F).T
     out["x5"] = fine5.astype(BF)
@@ -178,9 +180,22 @@
                     if 0 <= base + o < NY // factor:
                         along_y[r, y, first + o : first + planes * rows : rows] = table_y[fine, base + o]
         first += planes * rows
-    out["uz"] = along_z.reshape(SLABS * 16, ROWS_V).astype(np.float32)
-    out["uy"] = along_y.reshape(PENCILS * 40, ROWS_V).astype(np.float32)
+    out["uz"] = along_z.reshape(SLABS * 16, ROWS_V).astype(BF)
+    out["uy"] = np.pad(along_y, ((0, 0), (0, 8), (0, 0))).reshape(PENCILS * 48, ROWS_V).astype(BF)
     return out
+
+
+def bank_of(tables):
+    bank = np.zeros((BANK_ROWS, NX), BF)
+    place = {}
+    at = 0
+    for name, table in tables.items():
+        rows, width = table.shape
+        place[name] = (at, rows, -(-width // 128) * 128)
+        bank[at : at + rows, :width] = table
+        at += -(-rows // 16) * 16
+    assert at <= BANK_ROWS
+    return bank, place
 
 
 def pieces(value):
@@ -193,8 +208,9 @@
 
 
 def weighted(table_ref, height, high, low):
-    both = dot(table_ref[...], high)
-    return both[:height] + both[height:] + dot(table_ref[0:height, :], low)
+    count = high.shape[0]
+    both = dot(table_ref[:, 0:count], high)
+    return both[:height] + both[height:] + dot(table_ref[0:height, 0:count], low)
 
 
 def times_exact(value, exact):
@@ -204,16 +220,32 @@
     return both[:rows] + both[rows:]
 
 
+def fetches(sources, targets, sems):
+    copies = [
+        pltpu.make_async_copy(source, target, sems.at[i]) for i, (source, target) in enumerate(zip(sources, targets))
+    ]
+    for copy in copies:
+        copy.start()
+    return copies
+
+
 def shifted(value, step):
     lane = lax.broadcasted_iota(jnp.int32, value.shape, 1)
     rolled = pltpu.roll(value, (-step) % NX, 1)
     return jnp.where((lane + step >= 0) & (lane + step < NX), rolled, 0.0)
 
 
-def deposit_kernel(pos, cell, charge, block_sums, sums, up, down, far_up, far_down, copies, acc):
+def deposit_kernel(
+    blocks, pos, cell_hbm, charge_hbm, bank,
+    up, down, far_up, far_down, copies_hbm,
+    cell, charge, block_sums, sums, copies, acc, sems,
+):
     slab = pos[0]
     pencil = pos[1]
+    get = fetches((cell_hbm, charge_hbm, *blocks(bank)), (cell, charge, block_sums, sums), sems)
     acc[...] = jnp.zeros(acc.shape, F32)
+    get[0].wait()
+    get[1].wait()
 
     def step(block, carry):
         at = pl.ds(pl.multiple_of(block * BLOCK_A, BLOCK_A), BLOCK_A)
@@ -230,11 +262,18 @@
     lax.fori_loop(0, ATOMS_DEV // BLOCK_A, step, 0)
     down[0:128, :] = acc[0:128, :] + acc[256:384, :]
     up[0:128, :] = acc[128:256, :] + acc[384:512, :]
+    get[2].wait()
+    get[3].wait()
     high_down, low_down = pieces(down[0:128, :])
     high_up, low_up = pieces(up[0:128, :])
     stack = dot(block_sums[:, 0:128], high_down) + dot(block_sums[:, 128:256], high_up)
     stack = stack + dot(block_sums[:, 0:128], low_down) + dot(block_sums[:, 128:256], low_up)
     coarse = times_exact(stack, sums[...])
+    lane = lax.broadcasted_iota(jnp.int32, (2, 128), 1)
+    mine = jnp.where(lane < 64, coarse[80:82, 384:512], coarse[82:84, 384:512])
+    copies[...] = jnp.broadcast_to(mine[None], copies.shape)
+    send = pltpu.make_async_copy(copies, copies_hbm, sems.at[4])
+    send.start()
     for ref in (down, up):
         ref[128:160, 0:256] = coarse[0:32, 0:256]
         ref[128:160, 256:512] = coarse[32:64, 0:256]
@@ -243,9 +282,7 @@
         ref[160:168, 256:512] = jnp.zeros((8, 256), F32)
     far_down[...] = coarse[64:72, 256:384]
     far_up[...] = coarse[72:80, 256:384]
-    lane = lax.broadcasted_iota(jnp.int32, (2, 128), 1)
-    mine = jnp.where(lane < 64, coarse[80:82, 384:512], coarse[82:84, 384:512])
-    copies[...] = jnp.broadcast_to(mine[None], copies.shape)
+    send.wait()
 
 
 def planes_of(pos, down, up, below, above, far_below, far_above):
@@ -304,8 +341,11 @@
         to_left[88:96, lanes] = packed(level2(2 * t), level2(2 * t + 1), False)
 
 
-def coarse_fields(pos, level3, w3, w4, d3, d4, b5, x5, fields):
+def coarse_kernel(
+    blocks, pos, level3, bank, fields, w3, w4, d3, d4, b5, x5, sems
+):
     slab = pos[0]
+    get = fetches(blocks(bank), (w3, w4, d3, d4, b5, x5), sems)
 
     def slab_rows(index):
         inside = jnp.where((index >= 0) & (index < SLABS), 1.0, 0.0)
@@ -313,16 +353,18 @@
         return level3[pl.ds(at, 8), :] * inside
 
     blank = jnp.zeros((8, 128), F32)
+    for copy in get:
+        copy.wait()
     near3 = jnp.concatenate([slab_rows(slab - 3 + k) for k in range(7)] + [blank], 0)
     parts = weighted(w3, 288, *pieces(near3))
     wide = jnp.concatenate([parts[k * 48 : k * 48 + 48] for k in range(6)], 1)
-    fields[256:304, :] = times_exact(wide, d3[...])
+    fields[0:48, :] = times_exact(wide, d3[...])
     middle = 2 * (slab // 2)
     near4 = jnp.concatenate([slab_rows(middle - 6 + 2 * k) + slab_rows(middle - 5 + 2 * k) for k in range(7)] + [blank], 0)
     parts = weighted(w4, 144, *pieces(near4))
     wide = jnp.concatenate([parts[k * 24 : k * 24 + 24] for k in range(6)] , 1)
     wide = jnp.concatenate([wide, jnp.zeros((8, 768), F32)], 0)
-    fields[304:328, :] = times_exact(wide, d4[...])[0:24]
+    fields[48:72, :] = times_exact(wide, d4[...])[0:24]
     every = level3[...].reshape(16, 4, 8, 128)
     tops = jnp.sum(every, axis=1).reshape(128, 128)
     row = lax.broadcasted_iota(jnp.int32, (256, 128), 0)
@@ -336,18 +378,26 @@
     top_high, top_low = pieces(tops)
     parts = dot(kernel_high, top_high) + dot(kernel_low, top_high) + dot(kernel_high, top_low)
     wide = jnp.concatenate([parts[k * 16 : k * 16 + 16] for k in range(16)], 1)
-    fields[328:344, :] = times_exact(times_exact(wide, b5[...]), x5[...])
-    fields[344:384, :] = jnp.zeros((40, NX), F32)
+    narrow = [times_exact(wide[:, k * 512 : k * 512 + 512], b5[:, k * 128 : k * 128 + 128]) for k in range(4)]
+    fields[72:88, :] = times_exact(narrow[0] + narrow[1] + narrow[2] + narrow[3], x5[...])
+    fields[88:128, :] = jnp.zeros((40, NX), F32)
 
 
 def field_kernel(
-    pos, cell, charge, down, up, below, above, far_below, far_above, left, right, level3,
-    uz, uy, w0, w1, w2, w3, w4, d1, d2, d3, d4, b5, x5,
-    potential, forces,
-    high0, low0, high1, low1, high2, low2, fields, weights, wide1, wide2, grid, slopes,
+    blocks, place, pos, cell_hbm, charge_hbm, down, up, below, above, far_below, far_above, left, right, coarse, bank,
+    potential_hbm, forces,
+    cell, charge, uz, uy, w0, w1, w2, d1, d2, potential,
+    high0, low0, high1, low1, high2, low2, fields, weights, wide1, wide2, grid, slopes, sems,
 ):
     slab = pos[0]
     pencil = pos[1]
+    at_z = pl.multiple_of(place["uz"][0] + slab * 16, 16)
+    at_y = pl.multiple_of(place["uy"][0] + pencil * 48, 16)
+    get = fetches(
+        (*blocks(bank), bank.at[pl.ds(at_z, 16), 0:ROWS_V], bank.at[pl.ds(at_y, 48), 0:ROWS_V], cell_hbm, charge_hbm),
+        (w1, d1, w2, d2, w0, uz, uy, cell, charge),
+        sems,
+    )
     has_left = jnp.where(pencil > 0, 1.0, 0.0)
     has_right = jnp.where(pencil < PENCILS - 1, 1.0, 0.0)
     fine, level1, level2 = planes_of(pos, down, up, below, above, far_below, far_above)
@@ -384,7 +434,9 @@
         )
         high2[k * 32 : k * 32 + 32, :], low2[k * 32 : k * 32 + 32, :] = pieces(plane)
 
-    coarse_fields(pos, level3, w3, w4, d3, d4, b5, x5, fields)
+    fields[256:384, :] = coarse[...]
+    for copy in get[0:4]:
+        copy.wait()
     for o in range(8):
         parts = weighted(w1, 80, high1[o * 32 : o * 32 + 160, :], low1[o * 32 : o * 32 + 160, :])
         for c in range(3):
@@ -396,8 +448,12 @@
             wide2[o * 16 : o * 16 + 16, c * 128 : c * 128 + 128] = parts[c * 16 : c * 16 + 16]
     fields[192:256, :] = times_exact(wide2[...], d2[...])
 
+    for copy in get[4:9]:
+        copy.wait()
+    along_y = uy[0:48, :].astype(F32)[0:40]
+    along_z = uz[...].astype(F32)
     for z in range(12):
-        weights[z * 40 : z * 40 + 40, :] = uy[...] * uz[z : z + 1, :]
+        weights[z * 40 : z * 40 + 40, :] = along_y * along_z[z : z + 1]
     weight_high, weight_low = pieces(weights[...])
     field_high, field_low = pieces(fields[...])
     grid[...] = dot(weight_high, field_high) + dot(weight_low, field_high) + dot(weight_high, field_low)
@@ -435,6 +491,9 @@
             rows = slice(d * 256 + z * 32, d * 256 + z * 32 + 32)
             slopes[rows, 0:512], slopes[rows, 512:1024] = pieces(along[d])
 
+    put = pltpu.make_async_copy(potential, potential_hbm, sems.at[9])
+    put.start()
+
     def step(block, carry):
         at = pl.ds(pl.multiple_of(block * BLOCK_B, BLOCK_B), BLOCK_B)
         row = (cell[0:1, at] - slab * CZ) * CY + (cell[1:2, at] - pencil * CY)
@@ -448,10 +507,11 @@
         return carry
 
     lax.fori_loop(0, ATOMS_DEV // BLOCK_B, step, 0)
-
-
-def whole(count):
-    return [pl.BlockSpec(memory_space=pltpu.SMEM)] + [pl.BlockSpec(memory_space=pltpu.VMEM)] * count
+    put.wait()
+
+
+def specs(*spaces):
+    return [pl.BlockSpec(memory_space=space) for space, count in spaces for _ in range(count)]
 
 
 def rotated(value, slab_step, pencil_step):
@@ -468,46 +528,75 @@
 
 
 def make_body(tables):
-    params = pltpu.CompilerParams(vmem_limit_bytes=48 * 2**20)
+    bank_values, place = bank_of(tables)
+
+    def blocks(*names):
+        def take(bank):
+            return [bank.at[place[n][0] : place[n][0] + place[n][1], 0 : place[n][2]] for n in names]
+
+        return take
+
+    def room(*names):
+        return [pltpu.VMEM((place[n][1], place[n][2]), BF) for n in names]
 
     def body(atom_cell, charge):
         slab = lax.axis_index("slab")
         pencil = lax.axis_index("pencil")
         pos = jnp.stack([slab, pencil]).astype(jnp.int32)
         charge = charge.reshape(1, ATOMS_DEV)
+        bank = jnp.asarray(bank_values)
+        atoms = [pltpu.VMEM((3, ATOMS_DEV), jnp.int32), pltpu.VMEM((1, ATOMS_DEV), F32)]
         up, down, far_up, far_down, copies = pl.pallas_call(
-            deposit_kernel,
+            partial(deposit_kernel, blocks("block_sums", "sums")),
             out_shape=(f32_shape(168, NX), f32_shape(168, NX), f32_shape(8, 128), f32_shape(8, 128), f32_shape(256, 2, 128)),
-            in_specs=whole(4),
-            out_specs=[pl.BlockSpec(memory_space=pltpu.VMEM)] * 5,
-            scratch_shapes=[pltpu.VMEM((512, NX), F32)],
-            compiler_params=params,
+            in_specs=specs((pltpu.SMEM, 1), (pltpu.HBM, 3)),
+            out_specs=specs((pltpu.VMEM, 4), (pltpu.HBM, 1)),
+            scratch_shapes=[
+                *atoms,
+                *room("block_sums", "sums"),
+                pltpu.VMEM((256, 2, 128), F32),
+                pltpu.VMEM((512, NX), F32),
+                pltpu.SemaphoreType.DMA((5,)),
+            ],
+            compiler_params=pltpu.CompilerParams(vmem_limit_bytes=40 * 2**20),
             name="deposit",
-        )(pos, atom_cell, charge, jnp.asarray(tables["block_sums"]), jnp.asarray(tables["sums"]))
+        )(pos, atom_cell, charge, bank)
+        far_below = rotated(far_up, 2, 0)
+        far_above = rotated(far_down, -2, 0)
         below = rotated(up, 1, 0)
         above = rotated(down, -1, 0)
-        far_below = rotated(far_up, 2, 0)
-        far_above = rotated(far_down, -2, 0)
         level3 = lax.all_to_all(copies, BOTH, 0, 0, tiled=True).reshape(512, 128)
         to_right, to_left = pl.pallas_call(
             pack_kernel,
             out_shape=(f32_shape(96, NX), f32_shape(96, NX)),
-            in_specs=whole(6),
-            out_specs=[pl.BlockSpec(memory_space=pltpu.VMEM)] * 2,
-            compiler_params=params,
+            in_specs=specs((pltpu.SMEM, 1), (pltpu.VMEM, 6)),
+            out_specs=specs((pltpu.VMEM, 2)),
+            compiler_params=pltpu.CompilerParams(vmem_limit_bytes=8 * 2**20),
             name="pack",
         )(pos, down, up, below, above, far_below, far_above)
         left = rotated(to_right, 0, 1)
         right = rotated(to_left, 0, -1)
-        uz = lax.dynamic_slice_in_dim(jnp.asarray(tables["uz"]), slab * 16, 16, 0)
-        uy = lax.dynamic_slice_in_dim(jnp.asarray(tables["uy"]), pencil * 40, 40, 0)
-        names = ("w0", "w1", "w2", "w3", "w4", "d1", "d2", "d3", "d4", "b5", "x5")
+        wanted = ("w3", "w4", "d3", "d4", "b5", "x5")
+        coarse = pl.pallas_call(
+            partial(coarse_kernel, blocks(*wanted)),
+            out_shape=f32_shape(128, NX),
+            in_specs=specs((pltpu.SMEM, 1), (pltpu.VMEM, 1), (pltpu.HBM, 1)),
+            out_specs=pl.BlockSpec(memory_space=pltpu.VMEM),
+            scratch_shapes=[*room(*wanted), pltpu.SemaphoreType.DMA((6,))],
+            compiler_params=pltpu.CompilerParams(vmem_limit_bytes=40 * 2**20),
+            name="coarse",
+        )(pos, level3, bank)
         potential, forces = pl.pallas_call(
-            field_kernel,
+            partial(field_kernel, blocks("w1", "d1", "w2", "d2", "w0"), place),
             out_shape=(f32_shape(CZ * CY, NX), f32_shape(3, ATOMS_DEV)),
-            in_specs=whole(13 + len(names)),
-            out_specs=[pl.BlockSpec(memory_space=pltpu.VMEM)] * 2,
+            in_specs=specs((pltpu.SMEM, 1), (pltpu.HBM, 2), (pltpu.VMEM, 9), (pltpu.HBM, 1)),
+            out_specs=specs((pltpu.HBM, 1), (pltpu.VMEM, 1)),
             scratch_shapes=[
+                *atoms,
+                pltpu.VMEM((16, ROWS_V), BF),
+                pltpu.VMEM((48, ROWS_V), BF),
+                *room("w0", "w1", "w2", "d1", "d2"),
+                pltpu.VMEM((CZ * CY, NX), F32),
                 pltpu.VMEM((768, NX), BF),
                 pltpu.VMEM((768, NX), BF),
                 pltpu.VMEM((384, 256), BF),
@@ -520,12 +609,12 @@
                 pltpu.VMEM((64, 384), F32),
                 pltpu.VMEM((480, NX), F32),
                 pltpu.VMEM((768, 1024), BF),
+                pltpu.SemaphoreType.DMA((10,)),
             ],
-            compiler_params=params,
+            compiler_params=pltpu.CompilerParams(vmem_limit_bytes=40 * 2**20),
             name="field",
         )(
-            pos, atom_cell, charge, down, up, below, above, far_below, far_above, left, right, level3,
-            uz, uy, *[jnp.asarray(tables[name]) for name in names],
+            pos, atom_cell, charge, down, up, below, above, far_below, far_above, left, right, coarse, bank
         )
         return (potential.reshape(CZ, CY, NX), forces)
 

time: 86 us -> 72.4 us (0.84)
  local copies, waits for them, and re-layouts: 16.8 us -> 1.67 us
  Pallas kernels: 33 us -> 36.4 us
  waiting for transfers between devices: 8 us -> 6.57 us
    unnamed x46 -> x8, local copies, waits for them, and re-layouts: 14.6 us -> 1.67 us
    pallas_call x2 -> x3, Pallas kernels: 31.7 us -> 35.8 us  [the longest x1 24.2 us: body(): pl.pallas_call(partial(field_kernel, blocks('w1', 'd1', 'w2', 'd2', 'w0')...]
    dynamic_slice x2 -> x0, local copies, waits for them, and re-layouts: 2.18 us -> none  [the longest x1 1.35 us: body(): uz = lax.dynamic_slice_in_dim(jnp.asarray(tables['uz']), slab * 16, 16, 0)]
    ppermute x6, waiting for transfers between devices: 7.99 us -> 6.57 us  [rotated(): return lax.ppermute(value, BOTH, pairs)]
  transfers between devices with their start and end apart: 7 -> 7, of which waited for: 3 -> 3; matrix products, arithmetic and copies ran while one was open for 3% -> 0% of each run, Pallas kernels for 2% -> 6%
where the time goes in v2:
time: 72.4 us; the launch traced here: 72.1 us
  Pallas kernels  36.4 us (50%)
  starting transfers between devices  26.5 us (37%)
  waiting for transfers between devices  6.57 us (9%)
  local copies, waits for them, and re-layouts  1.67 us (2%)
  between operations  0.84 us (1%)
    pallas_call x1, Pallas kernels, body(): pl.pallas_call(partial(field_kernel, blocks('w1', 'd1', 'w2', 'd2', 'w0')...  24.2 us
    ppermute x6, starting transfers between devices, rotated(): return lax.ppermute(value, BOTH, pairs)  16.6 us
    all_to_all x1, starting transfers between devices, body(): level3 = lax.all_to_all(copies, BOTH, 0, 0, tiled=True).reshape(512, 128)  9.96 us
    pallas_call x1, Pallas kernels, body(): pl.pallas_call(partial(deposit_kernel, blocks('block_sums', 'sums')), out...  8.18 us
    ppermute x6, waiting for transfers between devices, rotated(): return lax.ppermute(value, BOTH, pairs)  6.57 us
    pallas_call x1, Pallas kernels, body(): pl.pallas_call(partial(coarse_kernel, blocks(*wanted)), out_shape=f32_sha...  3.45 us
    unnamed x8, local copies, waits for them, and re-layouts  1.67 us
  transfers between devices with their start and end apart: 7, of which 3 were waited for; matrix products, arithmetic and copies ran while one was open for 0% of the time, Pallas kernels for 6%

profile of v2, /device:TPU:24, one launch (start us, length us, event | category | flops | bytes accessed | tf_op | source)
XLA Modules:
  0.0 72.1 jit_solution(17042470738141870854)
XLA Ops:
  0.6 0.1 pad_add_fusion.pos
  0.7 0.0 copy-start
  0.7 0.9 %copy-done = s32[3,8192]{1,0:T(4,128)S(1)} copy-done((s32[3,8192]{1,0:T(4,128)S(1)}, s32[3,8192]{1,0:T(4,128)}, u32[]{:S(2)}) %copy-start) | copy-done | bytes 98328
  1.6 0.0 copy-start.2
  1.6 0.8 %copy-done.2 = f32[8192]{0:T(1024)S(1)} copy-done((f32[8192]{0:T(1024)S(1)}, f32[8192]{0:T(1024)}, u32[]{:S(2)}) %copy-start.2) | copy-done | bytes 32792
  2.4 0.0 copy-start.1
  2.4 0.0 copy-start.3
  2.4 8.2 %deposit.1 = (f32[168,512]{1,0:T(8,128)S(1)}, f32[168,512]{1,0:T(8,128)S(1)}, f32[8,128]{1,0:T(8,128)S(1)}, f32[8,128]{1,0:T(8,128)S(1)}, f32[256,2,128]{2,1,0:T(2,128)}) custom-call(s32[2]{0:T(128)S(1)} %pad_add_fusion.pos, s32[3,8192]{1,0:T(4,128)S(1)} %copy-done, f32[1,8192]{1,0:T(1,128)S(1)} %bitcast.6, bf16[28672,512]{1,0:T(8,128)(2,1)} %constant.11.clone.bank), custom_call_target="tpu_custom_call" | custom-call | tf_op jit(solution)/shard_map/deposit/pallas_call | solution.py:549
  10.6 7.6 %collective-permute-start.1 = (f32[168,512]{1,0:T(8,128)S(1)}, f32[168,512]{1,0:T(8,128)S(1)}, u32[]{:S(2)}, u32[]{:S(2)}) collective-permute-start(f32[168,512]{1,0:T(8,128)S(1)} %get-tuple-element.11.down), channel_id=1, source_target_pairs={{0,252},{1,253},{2,254},{3,255},{4,0},{5,1},{6,2},{7,3},{8,4},{9,5... | collective-permute-start | bytes 1032200 | tf_op jit(solution)/shard_map/ppermute | solution.py:523
  18.1 0.0 collective-permute-start
  18.1 10.0 %all-to-all-start = ((f32[256,2,128]{2,1,0:T(2,128)}), f32[256,2,128]{2,1,0:T(2,128)S(1)}, u32[]{:S(2)}, u32[]{:S(2)}) async-start(f32[256,2,128]{2,1,0:T(2,128)} %get-tuple-element.17), calls=%async_computation | async-start | bytes 524288 | tf_op jit(solution)/shard_map/all_to_all | solution.py:568
  28.1 1.6 %collective-permute-start.2 = (f32[8,128]{1,0:T(8,128)S(1)}, f32[8,128]{1,0:T(8,128)S(1)}, u32[]{:S(2)}, u32[]{:S(2)}) collective-permute-start(f32[8,128]{1,0:T(8,128)S(1)} %get-tuple-element.13), channel_id=1, source_target_pairs={{0,8},{1,9},{2,10},{3,11},{4,12},{5,13},{6,14},{7,15},{8,16},{9,17... | collective-permute-start | bytes 12296 | tf_op jit(solution)/shard_map/ppermute | solution.py:523
  29.7 5.3 %collective-permute-start.3 = (f32[8,128]{1,0:T(8,128)S(1)}, f32[8,128]{1,0:T(8,128)S(1)}, u32[]{:S(2)}, u32[]{:S(2)}) collective-permute-start(f32[8,128]{1,0:T(8,128)S(1)} %get-tuple-element.14), channel_id=1, source_target_pairs={{0,248},{1,249},{2,250},{3,251},{4,252},{5,253},{6,254},{7,255},{8... | collective-permute-start | bytes 12296 | tf_op jit(solution)/shard_map/ppermute | solution.py:523
  35.0 4.4 %collective-permute-done.2.far_below = f32[8,128]{1,0:T(8,128)S(1)} collective-permute-done((f32[8,128]{1,0:T(8,128)S(1)}, f32[8,128]{1,0:T(8,128)S(1)}, u32[]{:S(2)}, u32[]{:S(2)}) %collective-permute-start.2) | collective-permute-done | bytes 4128 | tf_op jit(solution)/shard_map/ppermute | solution.py:523
  39.4 0.0 collective-permute-done.3.far_above
  39.4 0.0 collective-permute-done.1.above
  39.4 0.0 collective-permute-done.below
  39.4 0.6 pack.1
  40.0 0.4 collective-permute-start.4
  40.4 1.7 %collective-permute-start.5 = (f32[96,512]{1,0:T(8,128)S(1)}, f32[96,512]{1,0:T(8,128)S(1)}, u32[]{:S(2)}, u32[]{:S(2)}) collective-permute-start(f32[96,512]{1,0:T(8,128)S(1)} %get-tuple-element.16), channel_id=1, source_target_pairs={{0,3},{1,0},{2,1},{3,2},{4,7},{5,4},{6,5},{7,6},{8,11},{9,8},{10,9... | collective-permute-start | bytes 589832 | tf_op jit(solution)/shard_map/ppermute | solution.py:523
  42.1 0.0 all-to-all-done
  42.1 3.5 %coarse.1 = f32[128,512]{1,0:T(8,128)S(1)} custom-call(s32[2]{0:T(128)S(1)} %pad_add_fusion.pos, f32[512,128]{1,0:T(8,128)S(1)} %bitcast.5, bf16[28672,512]{1,0:T(8,128)(2,1)} %constant.11.clone.bank), custom_call_target="tpu_custom_call" | custom-call | tf_op jit(solution)/shard_map/coarse/pallas_call | solution.py:580
  45.6 0.7 collective-permute-done.4.left
  46.2 1.5 %collective-permute-done.5.right = f32[96,512]{1,0:T(8,128)S(1)} collective-permute-done((f32[96,512]{1,0:T(8,128)S(1)}, f32[96,512]{1,0:T(8,128)S(1)}, u32[]{:S(2)}, u32[]{:S(2)}) %collective-permute-start.5) | collective-permute-done | bytes 196640 | tf_op jit(solution)/shard_map/ppermute | solution.py:523
  47.7 0.0 copy-done.1
  47.7 0.0 copy-done.3
  47.7 24.2 %field.1 = (f32[256,512]{1,0:T(8,128)}, f32[3,8192]{1,0:T(4,128)}) custom-call(s32[2]{0:T(128)S(1)} %pad_add_fusion.pos, s32[3,8192]{1,0:T(4,128)S(1)} %copy-done.1, f32[1,8192]{1,0:T(1,128)S(1)} %bitcast.7, f32[168,512]{1,0:T(8,128)S(1)} %get-tuple-element.11.down, f32[168,512]{1,0:T(8,128)S(1)} %get-tuple-element.12.up, ...), custom_call_target="tpu_custom_call" | custom-call | tf_op jit(solution)/shard_map/field/pallas_call | solution.py:589
Async XLA Ops:
  0.7 0.9 %copy-start = (s32[3,8192]{1,0:T(4,128)S(1)}, s32[3,8192]{1,0:T(4,128)}, u32[]{:S(2)}) copy-start(s32[3,8192]{1,0:T(4,128)} %cell_hbm.3) | copy-start | bytes 294916
  1.6 0.8 %copy-start.2 = (f32[8192]{0:T(1024)S(1)}, f32[8192]{0:T(1024)}, u32[]{:S(2)}) copy-start(f32[8192]{0:T(1024)} %param.4) | copy-start | bytes 98308
  2.4 45.4 %copy-start.1 = (s32[3,8192]{1,0:T(4,128)S(1)}, s32[3,8192]{1,0:T(4,128)}, u32[]{:S(2)}) copy-start(s32[3,8192]{1,0:T(4,128)} %cell_hbm.3) | copy-start | bytes 294916
  2.4 45.4 %copy-start.3 = (f32[8192]{0:T(1024)S(1)}, f32[8192]{0:T(1024)}, u32[]{:S(2)}) copy-start(f32[8192]{0:T(1024)} %param.4) | copy-start | bytes 98308
  10.6 28.8 %collective-permute-start.1 = (f32[168,512]{1,0:T(8,128)S(1)}, f32[168,512]{1,0:T(8,128)S(1)}, u32[]{:S(2)}, u32[]{:S(2)}) collective-permute-start(f32[168,512]{1,0:T(8,128)S(1)} %get-tuple-element.11.down), channel_id=1, source_target_pairs={{0,252},{1,253},{2,254},{3,255},{4,0},{5,1},{6,2},{7,3},{8,4},{9,5... | collective-permute-start | bytes 1032200 | tf_op jit(solution)/shard_map/ppermute | solution.py:523
  18.1 21.3 %collective-permute-start = (f32[168,512]{1,0:T(8,128)S(1)}, f32[168,512]{1,0:T(8,128)S(1)}, u32[]{:S(2)}, u32[]{:S(2)}) collective-permute-start(f32[168,512]{1,0:T(8,128)S(1)} %get-tuple-element.12.up), channel_id=1, source_target_pairs={{0,4},{1,5},{2,6},{3,7},{4,8},{5,9},{6,10},{7,11},{8,12},{9,13},{1... | collective-permute-start | bytes 1032200 | tf_op jit(solution)/shard_map/ppermute | solution.py:523
  18.1 24.0 %all-to-all-start = ((f32[256,2,128]{2,1,0:T(2,128)}), f32[256,2,128]{2,1,0:T(2,128)S(1)}, u32[]{:S(2)}, u32[]{:S(2)}) async-start(f32[256,2,128]{2,1,0:T(2,128)} %get-tuple-element.17), calls=%async_computation | async-start | bytes 524288 | tf_op jit(solution)/shard_map/all_to_all | solution.py:568
  28.1 11.3 %collective-permute-start.2 = (f32[8,128]{1,0:T(8,128)S(1)}, f32[8,128]{1,0:T(8,128)S(1)}, u32[]{:S(2)}, u32[]{:S(2)}) collective-permute-start(f32[8,128]{1,0:T(8,128)S(1)} %get-tuple-element.13), channel_id=1, source_target_pairs={{0,8},{1,9},{2,10},{3,11},{4,12},{5,13},{6,14},{7,15},{8,16},{9,17... | collective-permute-start | bytes 12296 | tf_op jit(solution)/shard_map/ppermute | solution.py:523
  29.7 9.7 %collective-permute-start.3 = (f32[8,128]{1,0:T(8,128)S(1)}, f32[8,128]{1,0:T(8,128)S(1)}, u32[]{:S(2)}, u32[]{:S(2)}) collective-permute-start(f32[8,128]{1,0:T(8,128)S(1)} %get-tuple-element.14), channel_id=1, source_target_pairs={{0,248},{1,249},{2,250},{3,251},{4,252},{5,253},{6,254},{7,255},{8... | collective-permute-start | bytes 12296 | tf_op jit(solution)/shard_map/ppermute | solution.py:523
  40.0 6.2 %collective-permute-start.4 = (f32[96,512]{1,0:T(8,128)S(1)}, f32[96,512]{1,0:T(8,128)S(1)}, u32[]{:S(2)}, u32[]{:S(2)}) collective-permute-start(f32[96,512]{1,0:T(8,128)S(1)} %get-tuple-element.15), channel_id=1, source_target_pairs={{0,1},{1,2},{2,3},{3,0},{4,5},{5,6},{6,7},{7,4},{8,9},{9,10},{10,1... | collective-permute-start | bytes 589832 | tf_op jit(solution)/shard_map/ppermute | solution.py:523
  40.4 7.3 %collective-permute-start.5 = (f32[96,512]{1,0:T(8,128)S(1)}, f32[96,512]{1,0:T(8,128)S(1)}, u32[]{:S(2)}, u32[]{:S(2)}) collective-permute-start(f32[96,512]{1,0:T(8,128)S(1)} %get-tuple-element.16), channel_id=1, source_target_pairs={{0,3},{1,0},{2,1},{3,2},{4,7},{5,4},{6,5},{7,6},{8,11},{9,8},{10,9... | collective-permute-start | bytes 589832 | tf_op jit(solution)/shard_map/ppermute | solution.py:523

commit v3 on v2

--- a/solution.py
+++ b/solution.py
@@ -22,9 +22,8 @@
 F32 = jnp.float32
 BOTH = ("slab", "pencil")
 ROWS_V = 384
-BLOCK_A = 1024
 BANK_ROWS = 28672
-BLOCK_B = 512
+BLOCK_B = 4096
 
 
 def near_weight(squared):
@@ -229,6 +228,15 @@
     return copies
 
 
+def columns_of(column):
+    count = column.shape[1]
+    high = jnp.broadcast_to(column >> 4, (16, count)).astype(jnp.int16)
+    low = jnp.broadcast_to(column & 15, (16, count))
+    part = jnp.where(lax.broadcasted_iota(jnp.int32, (16, count), 0) == low, 1.0, 0.0).astype(BF)
+    blank = jnp.zeros((16, count), BF)
+    return jnp.concatenate([jnp.where(high == jnp.int16(h), part, blank) for h in range(NX // 16)], 0)
+
+
 def shifted(value, step):
     lane = lax.broadcasted_iota(jnp.int32, value.shape, 1)
     rolled = pltpu.roll(value, (-step) % NX, 1)
@@ -236,34 +244,24 @@
 
 
 def deposit_kernel(
-    blocks, pos, cell_hbm, charge_hbm, bank,
+    blocks, pos, cell, charge, bank,
     up, down, far_up, far_down, copies_hbm,
-    cell, charge, block_sums, sums, copies, acc, sems,
+    block_sums, sums, copies, acc, sems,
 ):
     slab = pos[0]
     pencil = pos[1]
-    get = fetches((cell_hbm, charge_hbm, *blocks(bank)), (cell, charge, block_sums, sums), sems)
-    acc[...] = jnp.zeros(acc.shape, F32)
+    get = fetches(blocks(bank), (block_sums, sums), sems)
+    row = (cell[0:1, :] - slab * CZ) * CY + (cell[1:2, :] - pencil * CY)
+    high = charge[...].astype(BF).astype(F32)
+    low = charge[...] - high
+    here = lax.broadcasted_iota(jnp.int32, (CZ * CY, ATOMS_DEV), 0) == row
+    left = jnp.concatenate([jnp.where(here, high, 0.0).astype(BF), jnp.where(here, low, 0.0).astype(BF)], 0)
+    right = jnp.where(lax.broadcasted_iota(jnp.int32, (NX, ATOMS_DEV), 0) == cell[2:3, :], 1.0, 0.0).astype(BF)
+    acc[...] = lax.dot_general(left, right, (((1,), (1,)), ((), ())), preferred_element_type=F32)
+    down[0:128, :] = acc[0:128, :] + acc[256:384, :]
+    up[0:128, :] = acc[128:256, :] + acc[384:512, :]
     get[0].wait()
     get[1].wait()
-
-    def step(block, carry):
-        at = pl.ds(pl.multiple_of(block * BLOCK_A, BLOCK_A), BLOCK_A)
-        row = (cell[0:1, at] - slab * CZ) * CY + (cell[1:2, at] - pencil * CY)
-        column = cell[2:3, at]
-        high = charge[0:1, at].astype(BF).astype(F32)
-        low = charge[0:1, at] - high
-        here = lax.broadcasted_iota(jnp.int32, (CZ * CY, BLOCK_A), 0) == row
-        left = jnp.concatenate([jnp.where(here, high, 0.0).astype(BF), jnp.where(here, low, 0.0).astype(BF)], 0)
-        right = jnp.where(lax.broadcasted_iota(jnp.int32, (NX, BLOCK_A), 0) == column, 1.0, 0.0).astype(BF)
-        acc[...] += lax.dot_general(left, right, (((1,), (1,)), ((), ())), preferred_element_type=F32)
-        return carry
-
-    lax.fori_loop(0, ATOMS_DEV // BLOCK_A, step, 0)
-    down[0:128, :] = acc[0:128, :] + acc[256:384, :]
-    up[0:128, :] = acc[128:256, :] + acc[384:512, :]
-    get[2].wait()
-    get[3].wait()
     high_down, low_down = pieces(down[0:128, :])
     high_up, low_up = pieces(up[0:128, :])
     stack = dot(block_sums[:, 0:128], high_down) + dot(block_sums[:, 128:256], high_up)
@@ -272,7 +270,7 @@
     lane = lax.broadcasted_iota(jnp.int32, (2, 128), 1)
     mine = jnp.where(lane < 64, coarse[80:82, 384:512], coarse[82:84, 384:512])
     copies[...] = jnp.broadcast_to(mine[None], copies.shape)
-    send = pltpu.make_async_copy(copies, copies_hbm, sems.at[4])
+    send = pltpu.make_async_copy(copies, copies_hbm, sems.at[2])
     send.start()
     for ref in (down, up):
         ref[128:160, 0:256] = coarse[0:32, 0:256]
@@ -280,8 +278,8 @@
         ref[160:168, 0:128] = coarse[64:72, 256:384]
         ref[160:168, 128:256] = coarse[72:80, 256:384]
         ref[160:168, 256:512] = jnp.zeros((8, 256), F32)
-    far_down[...] = coarse[64:72, 256:384]
-    far_up[...] = coarse[72:80, 256:384]
+    far_down[0:8, :] = coarse[64:72, 256:384]
+    far_up[0:8, :] = coarse[72:80, 256:384]
     send.wait()
 
 
@@ -309,9 +307,9 @@
 
     def level2(k):
         if k == 0:
-            return far_below[...] * has_far_below
+            return far_below[0:8, :] * has_far_below
         if k == 7:
-            return far_above[...] * has_far_above
+            return far_above[0:8, :] * has_far_above
         ref, scale = (sources[0], sources[1], sources[3])[(k - 1) // 2]
         lane = (k - 1) % 2 * 128
         return masked(ref[160:168, lane : lane + 128], scale)
@@ -341,63 +339,68 @@
         to_left[88:96, lanes] = packed(level2(2 * t), level2(2 * t + 1), False)
 
 
-def coarse_kernel(
-    blocks, pos, level3, bank, fields, w3, w4, d3, d4, b5, x5, sems
-):
+def coarse_kernel(blocks, later, place, pos, level3, bank, *refs):
+    fields = refs[0]
+    kept = refs[1:8]
+    w3, w4, d3, d4, b5, x5, sems = refs[8:]
     slab = pos[0]
-    get = fetches(blocks(bank), (w3, w4, d3, d4, b5, x5), sems)
+    pencil = pos[1]
+    at_z = pl.multiple_of(place["uz"][0] + slab * 16, 16)
+    at_y = pl.multiple_of(place["uy"][0] + pencil * 48, 16)
+    get = fetches(
+        (*blocks(bank), *later(bank), bank.at[pl.ds(at_z, 16), 0:ROWS_V], bank.at[pl.ds(at_y, 48), 0:ROWS_V]),
+        (w3, w4, d3, d4, b5, x5, *kept),
+        sems,
+    )
 
     def slab_rows(index):
         inside = jnp.where((index >= 0) & (index < SLABS), 1.0, 0.0)
         at = pl.multiple_of(jnp.clip(index, 0, SLABS - 1) * 8, 8)
         return level3[pl.ds(at, 8), :] * inside
 
-    blank = jnp.zeros((8, 128), F32)
-    for copy in get:
-        copy.wait()
-    near3 = jnp.concatenate([slab_rows(slab - 3 + k) for k in range(7)] + [blank], 0)
-    parts = weighted(w3, 288, *pieces(near3))
-    wide = jnp.concatenate([parts[k * 48 : k * 48 + 48] for k in range(6)], 1)
-    fields[0:48, :] = times_exact(wide, d3[...])
-    middle = 2 * (slab // 2)
-    near4 = jnp.concatenate([slab_rows(middle - 6 + 2 * k) + slab_rows(middle - 5 + 2 * k) for k in range(7)] + [blank], 0)
-    parts = weighted(w4, 144, *pieces(near4))
-    wide = jnp.concatenate([parts[k * 24 : k * 24 + 24] for k in range(6)] , 1)
-    wide = jnp.concatenate([wide, jnp.zeros((8, 768), F32)], 0)
-    fields[48:72, :] = times_exact(wide, d4[...])[0:24]
     every = level3[...].reshape(16, 4, 8, 128)
     tops = jnp.sum(every, axis=1).reshape(128, 128)
     row = lax.broadcasted_iota(jnp.int32, (256, 128), 0)
     source = lax.broadcasted_iota(jnp.int32, (256, 128), 1)
     first_plane = jnp.clip(jnp.right_shift(16 * slab - 35, 6), 0, 13)
-    step_x = (row // 16).astype(F32)
-    step_z = (first_plane + row % 16 // 4 - source // 8).astype(F32)
-    step_y = (row % 4 - source % 8 // 2).astype(F32)
+    step_x = (row >> 4).astype(F32)
+    step_z = (first_plane + ((row & 15) >> 2) - (source >> 3)).astype(F32)
+    step_y = ((row & 3) - ((source & 7) >> 1)).astype(F32)
     kernel = (1.0 / F) / jnp.sqrt(step_z * step_z + step_y * step_y + step_x * step_x + 1.0)
     kernel_high, kernel_low = pieces(kernel)
     top_high, top_low = pieces(tops)
-    parts = dot(kernel_high, top_high) + dot(kernel_low, top_high) + dot(kernel_high, top_low)
-    wide = jnp.concatenate([parts[k * 16 : k * 16 + 16] for k in range(16)], 1)
+    parts5 = dot(kernel_high, top_high) + dot(kernel_low, top_high) + dot(kernel_high, top_low)
+    blank = jnp.zeros((8, 128), F32)
+    near3 = jnp.concatenate([slab_rows(slab - 3 + k) for k in range(7)] + [blank], 0)
+    middle = 2 * (slab // 2)
+    near4 = jnp.concatenate([slab_rows(middle - 6 + 2 * k) + slab_rows(middle - 5 + 2 * k) for k in range(7)] + [blank], 0)
+    get[0].wait()
+    get[1].wait()
+    parts3 = weighted(w3, 288, *pieces(near3))
+    parts4 = weighted(w4, 144, *pieces(near4))
+    for copy in get[2:6]:
+        copy.wait()
+    wide = jnp.concatenate([parts3[k * 48 : k * 48 + 48] for k in range(6)], 1)
+    fields[0:48, :] = times_exact(wide, d3[...])
+    wide = jnp.concatenate([parts4[k * 24 : k * 24 + 24] for k in range(6)], 1)
+    wide = jnp.concatenate([wide, jnp.zeros((8, 768), F32)], 0)
+    fields[48:72, :] = times_exact(wide, d4[...])[0:24]
+    wide = jnp.concatenate([parts5[k * 16 : k * 16 + 16] for k in range(16)], 1)
     narrow = [times_exact(wide[:, k * 512 : k * 512 + 512], b5[:, k * 128 : k * 128 + 128]) for k in range(4)]
     fields[72:88, :] = times_exact(narrow[0] + narrow[1] + narrow[2] + narrow[3], x5[...])
     fields[88:128, :] = jnp.zeros((40, NX), F32)
+    for copy in get[6:]:
+        copy.wait()
 
 
 def field_kernel(
-    blocks, place, pos, cell_hbm, charge_hbm, down, up, below, above, far_below, far_above, left, right, coarse, bank,
+    pos, cell, charge, down, up, below, above, far_below, far_above, left, right, coarse,
+    w0, w1, w2, d1, d2, uz, uy,
     potential_hbm, forces,
-    cell, charge, uz, uy, w0, w1, w2, d1, d2, potential,
-    high0, low0, high1, low1, high2, low2, fields, weights, wide1, wide2, grid, slopes, sems,
+    potential, high0, low0, high1, low1, high2, low2, fields, weights, wide1, wide2, grid, slopes, sems,
 ):
     slab = pos[0]
     pencil = pos[1]
-    at_z = pl.multiple_of(place["uz"][0] + slab * 16, 16)
-    at_y = pl.multiple_of(place["uy"][0] + pencil * 48, 16)
-    get = fetches(
-        (*blocks(bank), bank.at[pl.ds(at_z, 16), 0:ROWS_V], bank.at[pl.ds(at_y, 48), 0:ROWS_V], cell_hbm, charge_hbm),
-        (w1, d1, w2, d2, w0, uz, uy, cell, charge),
-        sems,
-    )
     has_left = jnp.where(pencil > 0, 1.0, 0.0)
     has_right = jnp.where(pencil < PENCILS - 1, 1.0, 0.0)
     fine, level1, level2 = planes_of(pos, down, up, below, above, far_below, far_above)
@@ -435,8 +438,6 @@
         high2[k * 32 : k * 32 + 32, :], low2[k * 32 : k * 32 + 32, :] = pieces(plane)
 
     fields[256:384, :] = coarse[...]
-    for copy in get[0:4]:
-        copy.wait()
     for o in range(8):
         parts = weighted(w1, 80, high1[o * 32 : o * 32 + 160, :], low1[o * 32 : o * 32 + 160, :])
         for c in range(3):
@@ -448,8 +449,6 @@
             wide2[o * 16 : o * 16 + 16, c * 128 : c * 128 + 128] = parts[c * 16 : c * 16 + 16]
     fields[192:256, :] = times_exact(wide2[...], d2[...])
 
-    for copy in get[4:9]:
-        copy.wait()
     along_y = uy[0:48, :].astype(F32)[0:40]
     along_z = uz[...].astype(F32)
     for z in range(12):
@@ -491,22 +490,23 @@
             rows = slice(d * 256 + z * 32, d * 256 + z * 32 + 32)
             slopes[rows, 0:512], slopes[rows, 512:1024] = pieces(along[d])
 
-    put = pltpu.make_async_copy(potential, potential_hbm, sems.at[9])
+    put = pltpu.make_async_copy(potential, potential_hbm, sems.at[0])
     put.start()
 
-    def step(block, carry):
-        at = pl.ds(pl.multiple_of(block * BLOCK_B, BLOCK_B), BLOCK_B)
+    for block in range(ATOMS_DEV // BLOCK_B):
+        at = slice(block * BLOCK_B, block * BLOCK_B + BLOCK_B)
         row = (cell[0:1, at] - slab * CZ) * CY + (cell[1:2, at] - pencil * CY)
-        column = cell[2:3, at]
-        chosen = jnp.where(lax.broadcasted_iota(jnp.int32, (NX, BLOCK_B), 0) == column, 1.0, 0.0).astype(BF)
+        chosen = columns_of(cell[2:3, at])
         lines = dot(slopes[...], jnp.concatenate([chosen, chosen], 0))
-        here = lax.broadcasted_iota(jnp.int32, (CZ * CY, BLOCK_B), 0) == row
+        row = jnp.broadcast_to(row, (8, BLOCK_B))
+        bits = [(row >> k) & 1 == 1 for k in range(3, 8)]
+        last = lax.broadcasted_iota(jnp.int32, (8, BLOCK_B), 0) == (row & 7)
         for d in range(3):
-            picked = jnp.sum(jnp.where(here, lines[d * 256 : d * 256 + 256], 0.0), axis=0, keepdims=True)
+            left = [lines[d * 256 + i * 8 : d * 256 + i * 8 + 8] for i in range(32)]
+            for bit in bits:
+                left = [jnp.where(bit, left[2 * i + 1], left[2 * i]) for i in range(len(left) // 2)]
+            picked = jnp.sum(jnp.where(last, left[0], 0.0), axis=0, keepdims=True)
             forces[d : d + 1, at] = -charge[0:1, at] * picked
-        return carry
-
-    lax.fori_loop(0, ATOMS_DEV // BLOCK_B, step, 0)
     put.wait()
 
 
@@ -545,18 +545,16 @@
         pos = jnp.stack([slab, pencil]).astype(jnp.int32)
         charge = charge.reshape(1, ATOMS_DEV)
         bank = jnp.asarray(bank_values)
-        atoms = [pltpu.VMEM((3, ATOMS_DEV), jnp.int32), pltpu.VMEM((1, ATOMS_DEV), F32)]
         up, down, far_up, far_down, copies = pl.pallas_call(
             partial(deposit_kernel, blocks("block_sums", "sums")),
             out_shape=(f32_shape(168, NX), f32_shape(168, NX), f32_shape(8, 128), f32_shape(8, 128), f32_shape(256, 2, 128)),
-            in_specs=specs((pltpu.SMEM, 1), (pltpu.HBM, 3)),
+            in_specs=specs((pltpu.SMEM, 1), (pltpu.VMEM, 2), (pltpu.HBM, 1)),
             out_specs=specs((pltpu.VMEM, 4), (pltpu.HBM, 1)),
             scratch_shapes=[
-                *atoms,
                 *room("block_sums", "sums"),
                 pltpu.VMEM((256, 2, 128), F32),
                 pltpu.VMEM((512, NX), F32),
-                pltpu.SemaphoreType.DMA((5,)),
+                pltpu.SemaphoreType.DMA((3,)),
             ],
             compiler_params=pltpu.CompilerParams(vmem_limit_bytes=40 * 2**20),
             name="deposit",
@@ -577,25 +575,27 @@
         left = rotated(to_right, 0, 1)
         right = rotated(to_left, 0, -1)
         wanted = ("w3", "w4", "d3", "d4", "b5", "x5")
-        coarse = pl.pallas_call(
-            partial(coarse_kernel, blocks(*wanted)),
-            out_shape=f32_shape(128, NX),
+        later = ("w0", "w1", "w2", "d1", "d2")
+        coarse, *kept = pl.pallas_call(
+            partial(coarse_kernel, blocks(*wanted), blocks(*later), place),
+            out_shape=(
+                f32_shape(128, NX),
+                *[jax.ShapeDtypeStruct((place[n][1], place[n][2]), BF) for n in later],
+                jax.ShapeDtypeStruct((16, ROWS_V), BF),
+                jax.ShapeDtypeStruct((48, ROWS_V), BF),
+            ),
             in_specs=specs((pltpu.SMEM, 1), (pltpu.VMEM, 1), (pltpu.HBM, 1)),
-            out_specs=pl.BlockSpec(memory_space=pltpu.VMEM),
-            scratch_shapes=[*room(*wanted), pltpu.SemaphoreType.DMA((6,))],
+            out_specs=specs((pltpu.VMEM, 8)),
+            scratch_shapes=[*room(*wanted), pltpu.SemaphoreType.DMA((13,))],
             compiler_params=pltpu.CompilerParams(vmem_limit_bytes=40 * 2**20),
             name="coarse",
         )(pos, level3, bank)
         potential, forces = pl.pallas_call(
-            partial(field_kernel, blocks("w1", "d1", "w2", "d2", "w0"), place),
+            field_kernel,
             out_shape=(f32_shape(CZ * CY, NX), f32_shape(3, ATOMS_DEV)),
-            in_specs=specs((pltpu.SMEM, 1), (pltpu.HBM, 2), (pltpu.VMEM, 9), (pltpu.HBM, 1)),
+            in_specs=specs((pltpu.SMEM, 1), (pltpu.VMEM, 18)),
             out_specs=specs((pltpu.HBM, 1), (pltpu.VMEM, 1)),
             scratch_shapes=[
-                *atoms,
-                pltpu.VMEM((16, ROWS_V), BF),
-                pltpu.VMEM((48, ROWS_V), BF),
-                *room("w0", "w1", "w2", "d1", "d2"),
                 pltpu.VMEM((CZ * CY, NX), F32),
                 pltpu.VMEM((768, NX), BF),
                 pltpu.VMEM((768, NX), BF),
@@ -609,12 +609,12 @@
                 pltpu.VMEM((64, 384), F32),
                 pltpu.VMEM((480, NX), F32),
                 pltpu.VMEM((768, 1024), BF),
-                pltpu.SemaphoreType.DMA((10,)),
+                pltpu.SemaphoreType.DMA((1,)),
             ],
             compiler_params=pltpu.CompilerParams(vmem_limit_bytes=40 * 2**20),
             name="field",
         )(
-            pos, atom_cell, charge, down, up, below, above, far_below, far_above, left, right, coarse, bank
+            pos, atom_cell, charge, down, up, below, above, far_below, far_above, left, right, coarse, *kept
         )
         return (potential.reshape(CZ, CY, NX), forces)
 

time: 72.4 us -> 65.6 us (0.906)
  Pallas kernels: 36.4 us -> 29.3 us
    pallas_call x2, Pallas kernels: 27.6 us -> 21.7 us  [the longest x1 18.7 us: body(): pl.pallas_call(field_kernel, out_shape=(f32_shape(CZ * CY, NX), f32_shape...]
    pallas_call x1, Pallas kernels: 8.18 us -> 6.95 us  [body(): pl.pallas_call(partial(deposit_kernel, blocks('block_sums', 'sums')), out...]
  transfers between devices with their start and end apart: 7 -> 7, of which waited for: 3 -> 3; matrix products, arithmetic and copies ran while one was open for 0% -> 0% of each run, Pallas kernels for 6% -> 5%
where the time goes in v3:
time: 65.6 us; the launch traced here: 65.4 us
  Pallas kernels  29.3 us (45%)
  starting transfers between devices  26.5 us (40%)
  waiting for transfers between devices  7.04 us (11%)
  local copies, waits for them, and re-layouts  1.67 us (3%)
  between operations  0.84 us (1%)
    pallas_call x1, Pallas kernels, body(): pl.pallas_call(field_kernel, out_shape=(f32_shape(CZ * CY, NX), f32_shape...  18.7 us
    ppermute x6, starting transfers between devices, rotated(): return lax.ppermute(value, BOTH, pairs)  16.6 us
    all_to_all x1, starting transfers between devices, body(): level3 = lax.all_to_all(copies, BOTH, 0, 0, tiled=True).reshape(512, 128)  9.97 us
    ppermute x6, waiting for transfers between devices, rotated(): return lax.ppermute(value, BOTH, pairs)  7.03 us
    pallas_call x1, Pallas kernels, body(): pl.pallas_call(partial(deposit_kernel, blocks('block_sums', 'sums')), out...  6.95 us
    pallas_call x1, Pallas kernels, body(): pl.pallas_call(partial(coarse_kernel, blocks(*wanted), blocks(*later), pl...  2.98 us
    unnamed x8, local copies, waits for them, and re-layouts  1.67 us
  transfers between devices with their start and end apart: 7, of which 3 were waited for; matrix products, arithmetic and copies ran while one was open for 0% of the time, Pallas kernels for 5%

profile of v3, /device:TPU:24, one launch (start us, length us, event | category | flops | bytes accessed | tf_op | source)
XLA Modules:
  0.0 65.4 jit_solution(15524457218111607471)
XLA Ops:
  0.6 0.1 pad_add_fusion.pos
  0.7 0.0 copy-start
  0.7 0.9 %copy-done = s32[3,8192]{1,0:T(4,128)S(1)} copy-done((s32[3,8192]{1,0:T(4,128)S(1)}, s32[3,8192]{1,0:T(4,128)}, u32[]{:S(2)}) %copy-start) | copy-done | bytes 98328
  1.6 0.0 copy-start.2
  1.6 0.8 %copy-done.2 = f32[8192]{0:T(1024)S(1)} copy-done((f32[8192]{0:T(1024)S(1)}, f32[8192]{0:T(1024)}, u32[]{:S(2)}) %copy-start.2) | copy-done | bytes 32792
  2.4 0.0 copy-start.1
  2.4 0.0 copy-start.3
  2.4 6.9 %deposit.1 = (f32[168,512]{1,0:T(8,128)S(1)}, f32[168,512]{1,0:T(8,128)S(1)}, f32[8,128]{1,0:T(8,128)S(1)}, f32[8,128]{1,0:T(8,128)S(1)}, f32[256,2,128]{2,1,0:T(2,128)}) custom-call(s32[2]{0:T(128)S(1)} %pad_add_fusion.pos, s32[3,8192]{1,0:T(4,128)S(1)} %copy-done, f32[1,8192]{1,0:T(1,128)S(1)} %bitcast.6, bf16[28672,512]{1,0:T(8,128)(2,1)} %constant.11.clone.bank), custom_call_target="tpu_custom_call" | custom-call | tf_op jit(solution)/shard_map/deposit/pallas_call | solution.py:548
  9.3 7.6 %collective-permute-start.1 = (f32[168,512]{1,0:T(8,128)S(1)}, f32[168,512]{1,0:T(8,128)S(1)}, u32[]{:S(2)}, u32[]{:S(2)}) collective-permute-start(f32[168,512]{1,0:T(8,128)S(1)} %get-tuple-element.19.down), channel_id=1, source_target_pairs={{0,252},{1,253},{2,254},{3,255},{4,0},{5,1},{6,2},{7,3},{8,4},{9,5... | collective-permute-start | bytes 1032200 | tf_op jit(solution)/shard_map/ppermute | solution.py:523
  16.9 0.0 collective-permute-start
  16.9 10.0 %all-to-all-start = ((f32[256,2,128]{2,1,0:T(2,128)}), f32[256,2,128]{2,1,0:T(2,128)S(1)}, u32[]{:S(2)}, u32[]{:S(2)}) async-start(f32[256,2,128]{2,1,0:T(2,128)} %get-tuple-element.25), calls=%async_computation | async-start | bytes 524288 | tf_op jit(solution)/shard_map/all_to_all | solution.py:566
  26.9 1.6 %collective-permute-start.2 = (f32[8,128]{1,0:T(8,128)S(1)}, f32[8,128]{1,0:T(8,128)S(1)}, u32[]{:S(2)}, u32[]{:S(2)}) collective-permute-start(f32[8,128]{1,0:T(8,128)S(1)} %get-tuple-element.21), channel_id=1, source_target_pairs={{0,8},{1,9},{2,10},{3,11},{4,12},{5,13},{6,14},{7,15},{8,16},{9,17... | collective-permute-start | bytes 12296 | tf_op jit(solution)/shard_map/ppermute | solution.py:523
  28.4 5.3 %collective-permute-start.3 = (f32[8,128]{1,0:T(8,128)S(1)}, f32[8,128]{1,0:T(8,128)S(1)}, u32[]{:S(2)}, u32[]{:S(2)}) collective-permute-start(f32[8,128]{1,0:T(8,128)S(1)} %get-tuple-element.22), channel_id=1, source_target_pairs={{0,248},{1,249},{2,250},{3,251},{4,252},{5,253},{6,254},{7,255},{8... | collective-permute-start | bytes 12296 | tf_op jit(solution)/shard_map/ppermute | solution.py:523
  33.8 4.4 %collective-permute-done.2.far_below = f32[8,128]{1,0:T(8,128)S(1)} collective-permute-done((f32[8,128]{1,0:T(8,128)S(1)}, f32[8,128]{1,0:T(8,128)S(1)}, u32[]{:S(2)}, u32[]{:S(2)}) %collective-permute-start.2) | collective-permute-done | bytes 4128 | tf_op jit(solution)/shard_map/ppermute | solution.py:523
  38.2 0.0 collective-permute-done.3.far_above
  38.2 0.0 collective-permute-done.1.above
  38.2 0.0 collective-permute-done.below
  38.2 0.6 pack.1
  38.8 0.4 collective-permute-start.4
  39.2 1.7 %collective-permute-start.5 = (f32[96,512]{1,0:T(8,128)S(1)}, f32[96,512]{1,0:T(8,128)S(1)}, u32[]{:S(2)}, u32[]{:S(2)}) collective-permute-start(f32[96,512]{1,0:T(8,128)S(1)} %get-tuple-element.24), channel_id=1, source_target_pairs={{0,3},{1,0},{2,1},{3,2},{4,7},{5,4},{6,5},{7,6},{8,11},{9,8},{10,9... | collective-permute-start | bytes 589832 | tf_op jit(solution)/shard_map/ppermute | solution.py:523
  40.9 0.0 all-to-all-done
  40.9 3.0 %coarse.1 = (f32[128,512]{1,0:T(8,128)S(1)}, bf16[256,256]{1,0:T(8,128)(2,1)S(1)}, bf16[160,256]{1,0:T(8,128)(2,1)S(1)}, bf16[96,256]{1,0:T(8,128)(2,1)S(1)}, bf...) custom-call(s32[2]{0:T(128)S(1)} %pad_add_fusion.pos, ...), custom_call_target="tpu_custom_call" | custom-call | tf_op jit(solution)/shard_map/coarse/pallas_call | solution.py:579
  43.9 1.1 %collective-permute-done.4.left = f32[96,512]{1,0:T(8,128)S(1)} collective-permute-done((f32[96,512]{1,0:T(8,128)S(1)}, f32[96,512]{1,0:T(8,128)S(1)}, u32[]{:S(2)}, u32[]{:S(2)}) %collective-permute-start.4) | collective-permute-done | bytes 196640 | tf_op jit(solution)/shard_map/ppermute | solution.py:523
  45.0 1.5 %collective-permute-done.5.right = f32[96,512]{1,0:T(8,128)S(1)} collective-permute-done((f32[96,512]{1,0:T(8,128)S(1)}, f32[96,512]{1,0:T(8,128)S(1)}, u32[]{:S(2)}, u32[]{:S(2)}) %collective-permute-start.5) | collective-permute-done | bytes 196640 | tf_op jit(solution)/shard_map/ppermute | solution.py:523
  46.5 0.0 copy-done.1
  46.5 0.0 copy-done.3
  46.5 18.7 %field.1 = (f32[256,512]{1,0:T(8,128)}, f32[3,8192]{1,0:T(4,128)}) custom-call(s32[2]{0:T(128)S(1)} %pad_add_fusion.pos, s32[3,8192]{1,0:T(4,128)S(1)} %copy-done.1, f32[1,8192]{1,0:T(1,128)S(1)} %bitcast.7, f32[168,512]{1,0:T(8,128)S(1)} %get-tuple-element.19.down, f32[168,512]{1,0:T(8,128)S(1)} %get-tuple-element.20.up, ...), custom_call_target="tpu_custom_call" | custom-call | tf_op jit(solution)/shard_map/field/pallas_call | solution.py:593
Async XLA Ops:
  0.7 0.9 %copy-start = (s32[3,8192]{1,0:T(4,128)S(1)}, s32[3,8192]{1,0:T(4,128)}, u32[]{:S(2)}) copy-start(s32[3,8192]{1,0:T(4,128)} %cell.3) | copy-start | bytes 294916
  1.6 0.8 %copy-start.2 = (f32[8192]{0:T(1024)S(1)}, f32[8192]{0:T(1024)}, u32[]{:S(2)}) copy-start(f32[8192]{0:T(1024)} %param.4) | copy-start | bytes 98308
  2.4 44.1 %copy-start.1 = (s32[3,8192]{1,0:T(4,128)S(1)}, s32[3,8192]{1,0:T(4,128)}, u32[]{:S(2)}) copy-start(s32[3,8192]{1,0:T(4,128)} %cell.3) | copy-start | bytes 294916
  2.4 44.1 %copy-start.3 = (f32[8192]{0:T(1024)S(1)}, f32[8192]{0:T(1024)}, u32[]{:S(2)}) copy-start(f32[8192]{0:T(1024)} %param.4) | copy-start | bytes 98308
  9.3 28.9 %collective-permute-start.1 = (f32[168,512]{1,0:T(8,128)S(1)}, f32[168,512]{1,0:T(8,128)S(1)}, u32[]{:S(2)}, u32[]{:S(2)}) collective-permute-start(f32[168,512]{1,0:T(8,128)S(1)} %get-tuple-element.19.down), channel_id=1, source_target_pairs={{0,252},{1,253},{2,254},{3,255},{4,0},{5,1},{6,2},{7,3},{8,4},{9,5... | collective-permute-start | bytes 1032200 | tf_op jit(solution)/shard_map/ppermute | solution.py:523
  16.9 21.3 %collective-permute-start = (f32[168,512]{1,0:T(8,128)S(1)}, f32[168,512]{1,0:T(8,128)S(1)}, u32[]{:S(2)}, u32[]{:S(2)}) collective-permute-start(f32[168,512]{1,0:T(8,128)S(1)} %get-tuple-element.20.up), channel_id=1, source_target_pairs={{0,4},{1,5},{2,6},{3,7},{4,8},{5,9},{6,10},{7,11},{8,12},{9,13},{1... | collective-permute-start | bytes 1032200 | tf_op jit(solution)/shard_map/ppermute | solution.py:523
  16.9 24.0 %all-to-all-start = ((f32[256,2,128]{2,1,0:T(2,128)}), f32[256,2,128]{2,1,0:T(2,128)S(1)}, u32[]{:S(2)}, u32[]{:S(2)}) async-start(f32[256,2,128]{2,1,0:T(2,128)} %get-tuple-element.25), calls=%async_computation | async-start | bytes 524288 | tf_op jit(solution)/shard_map/all_to_all | solution.py:566
  26.9 11.3 %collective-permute-start.2 = (f32[8,128]{1,0:T(8,128)S(1)}, f32[8,128]{1,0:T(8,128)S(1)}, u32[]{:S(2)}, u32[]{:S(2)}) collective-permute-start(f32[8,128]{1,0:T(8,128)S(1)} %get-tuple-element.21), channel_id=1, source_target_pairs={{0,8},{1,9},{2,10},{3,11},{4,12},{5,13},{6,14},{7,15},{8,16},{9,17... | collective-permute-start | bytes 12296 | tf_op jit(solution)/shard_map/ppermute | solution.py:523
  28.4 9.7 %collective-permute-start.3 = (f32[8,128]{1,0:T(8,128)S(1)}, f32[8,128]{1,0:T(8,128)S(1)}, u32[]{:S(2)}, u32[]{:S(2)}) collective-permute-start(f32[8,128]{1,0:T(8,128)S(1)} %get-tuple-element.22), channel_id=1, source_target_pairs={{0,248},{1,249},{2,250},{3,251},{4,252},{5,253},{6,254},{7,255},{8... | collective-permute-start | bytes 12296 | tf_op jit(solution)/shard_map/ppermute | solution.py:523
  38.8 6.2 %collective-permute-start.4 = (f32[96,512]{1,0:T(8,128)S(1)}, f32[96,512]{1,0:T(8,128)S(1)}, u32[]{:S(2)}, u32[]{:S(2)}) collective-permute-start(f32[96,512]{1,0:T(8,128)S(1)} %get-tuple-element.23), channel_id=1, source_target_pairs={{0,1},{1,2},{2,3},{3,0},{4,5},{5,6},{6,7},{7,4},{8,9},{9,10},{10,1... | collective-permute-start | bytes 589832 | tf_op jit(solution)/shard_map/ppermute | solution.py:523
  39.2 7.3 %collective-permute-start.5 = (f32[96,512]{1,0:T(8,128)S(1)}, f32[96,512]{1,0:T(8,128)S(1)}, u32[]{:S(2)}, u32[]{:S(2)}) collective-permute-start(f32[96,512]{1,0:T(8,128)S(1)} %get-tuple-element.24), channel_id=1, source_target_pairs={{0,3},{1,0},{2,1},{3,2},{4,7},{5,4},{6,5},{7,6},{8,11},{9,8},{10,9... | collective-permute-start | bytes 589832 | tf_op jit(solution)/shard_map/ppermute | solution.py:523

commit v4 on v3

--- a/solution.py
+++ b/solution.py
@@ -115,9 +115,7 @@
     out = []
     x3 = np.arange(128) % 64
     for block in spread(level):
-        for j in range(2):
-            keep = (np.arange(128) // 64 == j)[:, None]
-            out.append(np.where(keep, block[x3 >> (level - 3)], 0.0))
+        out.append(block[x3 >> (level - 3)])
     return np.concatenate(out, 0)
 
 
@@ -380,10 +378,16 @@
     parts4 = weighted(w4, 144, *pieces(near4))
     for copy in get[2:6]:
         copy.wait()
-    wide = jnp.concatenate([parts3[k * 48 : k * 48 + 48] for k in range(6)], 1)
+    first_half = lax.broadcasted_iota(jnp.int32, (48, 128), 1) < 64
+    wide = jnp.concatenate(
+        [jnp.where(first_half, parts3[k * 96 : k * 96 + 48], parts3[k * 96 + 48 : k * 96 + 96]) for k in range(3)], 1
+    )
     fields[0:48, :] = times_exact(wide, d3[...])
-    wide = jnp.concatenate([parts4[k * 24 : k * 24 + 24] for k in range(6)], 1)
-    wide = jnp.concatenate([wide, jnp.zeros((8, 768), F32)], 0)
+    first_half = first_half[0:24]
+    wide = jnp.concatenate(
+        [jnp.where(first_half, parts4[k * 48 : k * 48 + 24], parts4[k * 48 + 24 : k * 48 + 48]) for k in range(3)], 1
+    )
+    wide = jnp.concatenate([wide, jnp.zeros((8, 384), F32)], 0)
     fields[48:72, :] = times_exact(wide, d4[...])[0:24]
     wide = jnp.concatenate([parts5[k * 16 : k * 16 + 16] for k in range(16)], 1)
     narrow = [times_exact(wide[:, k * 512 : k * 512 + 512], b5[:, k * 128 : k * 128 + 128]) for k in range(4)]
@@ -396,8 +400,8 @@
 def field_kernel(
     pos, cell, charge, down, up, below, above, far_below, far_above, left, right, coarse,
     w0, w1, w2, d1, d2, uz, uy,
-    potential_hbm, forces,
-    potential, high0, low0, high1, low1, high2, low2, fields, weights, wide1, wide2, grid, slopes, sems,
+    potential_hbm, forces_hbm,
+    potential, forces, high0, low0, high1, low1, high2, low2, fields, weights, wide1, wide2, grid, slopes, sems,
 ):
     slab = pos[0]
     pencil = pos[1]
@@ -492,6 +496,7 @@
 
     put = pltpu.make_async_copy(potential, potential_hbm, sems.at[0])
     put.start()
+    puts = [put]
 
     for block in range(ATOMS_DEV // BLOCK_B):
         at = slice(block * BLOCK_B, block * BLOCK_B + BLOCK_B)
@@ -507,7 +512,10 @@
                 left = [jnp.where(bit, left[2 * i + 1], left[2 * i]) for i in range(len(left) // 2)]
             picked = jnp.sum(jnp.where(last, left[0], 0.0), axis=0, keepdims=True)
             forces[d : d + 1, at] = -charge[0:1, at] * picked
-    put.wait()
+        puts.append(pltpu.make_async_copy(forces.at[:, at], forces_hbm.at[:, at], sems.at[1 + block]))
+        puts[-1].start()
+    for put in puts:
+        put.wait()
 
 
 def specs(*spaces):
@@ -594,9 +602,10 @@
             field_kernel,
             out_shape=(f32_shape(CZ * CY, NX), f32_shape(3, ATOMS_DEV)),
             in_specs=specs((pltpu.SMEM, 1), (pltpu.VMEM, 18)),
-            out_specs=specs((pltpu.HBM, 1), (pltpu.VMEM, 1)),
+            out_specs=specs((pltpu.HBM, 2)),
             scratch_shapes=[
                 pltpu.VMEM((CZ * CY, NX), F32),
+                pltpu.VMEM((3, ATOMS_DEV), F32),
                 pltpu.VMEM((768, NX), BF),
                 pltpu.VMEM((768, NX), BF),
                 pltpu.VMEM((384, 256), BF),
@@ -609,7 +618,7 @@
                 pltpu.VMEM((64, 384), F32),
                 pltpu.VMEM((480, NX), F32),
                 pltpu.VMEM((768, 1024), BF),
-                pltpu.SemaphoreType.DMA((1,)),
+                pltpu.SemaphoreType.DMA((1 + ATOMS_DEV // BLOCK_B,)),
             ],
             compiler_params=pltpu.CompilerParams(vmem_limit_bytes=40 * 2**20),
             name="field",

time: 65.6 us -> 65.6 us (level)
  no operation moved by 1% of the time
where the time goes in v4:
time: 65.6 us; the launch traced here: 65.4 us
  Pallas kernels  28.9 us (44%)
  starting transfers between devices  26.5 us (40%)
  waiting for transfers between devices  7.39 us (11%)
  local copies, waits for them, and re-layouts  1.67 us (3%)
  between operations  0.84 us (1%)
    pallas_call x1, Pallas kernels, body(): pl.pallas_call(field_kernel, out_shape=(f32_shape(CZ * CY, NX), f32_shape...  18.7 us
    ppermute x6, starting transfers between devices, rotated(): return lax.ppermute(value, BOTH, pairs)  16.6 us
    all_to_all x1, starting transfers between devices, body(): level3 = lax.all_to_all(copies, BOTH, 0, 0, tiled=True).reshape(512, 128)  9.97 us
    ppermute x6, waiting for transfers between devices, rotated(): return lax.ppermute(value, BOTH, pairs)  7.39 us
    pallas_call x1, Pallas kernels, body(): pl.pallas_call(partial(deposit_kernel, blocks('block_sums', 'sums')), out...  6.95 us
    pallas_call x1, Pallas kernels, body(): pl.pallas_call(partial(coarse_kernel, blocks(*wanted), blocks(*later), pl...  2.63 us
    unnamed x8, local copies, waits for them, and re-layouts  1.67 us
  transfers between devices with their start and end apart: 7, of which 3 were waited for; matrix products, arithmetic and copies ran while one was open for 0% of the time, Pallas kernels for 5%

profile of v4, /device:TPU:24, one launch (start us, length us, event | category | flops | bytes accessed | tf_op | source)
XLA Modules:
  0.0 65.4 jit_solution(15027203657519819232)
XLA Ops:
  0.6 0.1 pad_add_fusion.pos
  0.7 0.0 copy-start
  0.7 0.9 %copy-done = s32[3,8192]{1,0:T(4,128)S(1)} copy-done((s32[3,8192]{1,0:T(4,128)S(1)}, s32[3,8192]{1,0:T(4,128)}, u32[]{:S(2)}) %copy-start) | copy-done | bytes 98328
  1.6 0.0 copy-start.2
  1.6 0.8 %copy-done.2 = f32[8192]{0:T(1024)S(1)} copy-done((f32[8192]{0:T(1024)S(1)}, f32[8192]{0:T(1024)}, u32[]{:S(2)}) %copy-start.2) | copy-done | bytes 32792
  2.4 0.0 copy-start.1
  2.4 0.0 copy-start.3
  2.4 6.9 %deposit.1 = (f32[168,512]{1,0:T(8,128)S(1)}, f32[168,512]{1,0:T(8,128)S(1)}, f32[8,128]{1,0:T(8,128)S(1)}, f32[8,128]{1,0:T(8,128)S(1)}, f32[256,2,128]{2,1,0:T(2,128)}) custom-call(s32[2]{0:T(128)S(1)} %pad_add_fusion.pos, s32[3,8192]{1,0:T(4,128)S(1)} %copy-done, f32[1,8192]{1,0:T(1,128)S(1)} %bitcast.6, bf16[28672,512]{1,0:T(8,128)(2,1)} %constant.11.clone.bank), custom_call_target="tpu_custom_call" | custom-call | tf_op jit(solution)/shard_map/deposit/pallas_call | solution.py:556
  9.3 7.6 %collective-permute-start.1 = (f32[168,512]{1,0:T(8,128)S(1)}, f32[168,512]{1,0:T(8,128)S(1)}, u32[]{:S(2)}, u32[]{:S(2)}) collective-permute-start(f32[168,512]{1,0:T(8,128)S(1)} %get-tuple-element.19.down), channel_id=1, source_target_pairs={{0,252},{1,253},{2,254},{3,255},{4,0},{5,1},{6,2},{7,3},{8,4},{9,5... | collective-permute-start | bytes 1032200 | tf_op jit(solution)/shard_map/ppermute | solution.py:531
  16.9 0.0 collective-permute-start
  16.9 10.0 %all-to-all-start = ((f32[256,2,128]{2,1,0:T(2,128)}), f32[256,2,128]{2,1,0:T(2,128)S(1)}, u32[]{:S(2)}, u32[]{:S(2)}) async-start(f32[256,2,128]{2,1,0:T(2,128)} %get-tuple-element.25), calls=%async_computation | async-start | bytes 524288 | tf_op jit(solution)/shard_map/all_to_all | solution.py:574
  26.9 1.6 %collective-permute-start.2 = (f32[8,128]{1,0:T(8,128)S(1)}, f32[8,128]{1,0:T(8,128)S(1)}, u32[]{:S(2)}, u32[]{:S(2)}) collective-permute-start(f32[8,128]{1,0:T(8,128)S(1)} %get-tuple-element.21), channel_id=1, source_target_pairs={{0,8},{1,9},{2,10},{3,11},{4,12},{5,13},{6,14},{7,15},{8,16},{9,17... | collective-permute-start | bytes 12296 | tf_op jit(solution)/shard_map/ppermute | solution.py:531
  28.4 5.3 %collective-permute-start.3 = (f32[8,128]{1,0:T(8,128)S(1)}, f32[8,128]{1,0:T(8,128)S(1)}, u32[]{:S(2)}, u32[]{:S(2)}) collective-permute-start(f32[8,128]{1,0:T(8,128)S(1)} %get-tuple-element.22), channel_id=1, source_target_pairs={{0,248},{1,249},{2,250},{3,251},{4,252},{5,253},{6,254},{7,255},{8... | collective-permute-start | bytes 12296 | tf_op jit(solution)/shard_map/ppermute | solution.py:531
  33.8 4.4 %collective-permute-done.2.far_below = f32[8,128]{1,0:T(8,128)S(1)} collective-permute-done((f32[8,128]{1,0:T(8,128)S(1)}, f32[8,128]{1,0:T(8,128)S(1)}, u32[]{:S(2)}, u32[]{:S(2)}) %collective-permute-start.2) | collective-permute-done | bytes 4128 | tf_op jit(solution)/shard_map/ppermute | solution.py:531
  38.2 0.0 collective-permute-done.3.far_above
  38.2 0.0 collective-permute-done.1.above
  38.2 0.0 collective-permute-done.below
  38.2 0.6 pack.1
  38.8 0.4 collective-permute-start.4
  39.2 1.7 %collective-permute-start.5 = (f32[96,512]{1,0:T(8,128)S(1)}, f32[96,512]{1,0:T(8,128)S(1)}, u32[]{:S(2)}, u32[]{:S(2)}) collective-permute-start(f32[96,512]{1,0:T(8,128)S(1)} %get-tuple-element.24), channel_id=1, source_target_pairs={{0,3},{1,0},{2,1},{3,2},{4,7},{5,4},{6,5},{7,6},{8,11},{9,8},{10,9... | collective-permute-start | bytes 589832 | tf_op jit(solution)/shard_map/ppermute | solution.py:531
  40.9 0.0 all-to-all-done
  40.9 2.6 %coarse.1 = (f32[128,512]{1,0:T(8,128)S(1)}, bf16[256,256]{1,0:T(8,128)(2,1)S(1)}, bf16[160,256]{1,0:T(8,128)(2,1)S(1)}, bf16[96,256]{1,0:T(8,128)(2,1)S(1)}, bf...) custom-call(s32[2]{0:T(128)S(1)} %pad_add_fusion.pos, ...), custom_call_target="tpu_custom_call" | custom-call | tf_op jit(solution)/shard_map/coarse/pallas_call | solution.py:587
  43.5 1.5 %collective-permute-done.4.left = f32[96,512]{1,0:T(8,128)S(1)} collective-permute-done((f32[96,512]{1,0:T(8,128)S(1)}, f32[96,512]{1,0:T(8,128)S(1)}, u32[]{:S(2)}, u32[]{:S(2)}) %collective-permute-start.4) | collective-permute-done | bytes 196640 | tf_op jit(solution)/shard_map/ppermute | solution.py:531
  45.0 1.5 %collective-permute-done.5.right = f32[96,512]{1,0:T(8,128)S(1)} collective-permute-done((f32[96,512]{1,0:T(8,128)S(1)}, f32[96,512]{1,0:T(8,128)S(1)}, u32[]{:S(2)}, u32[]{:S(2)}) %collective-permute-start.5) | collective-permute-done | bytes 196640 | tf_op jit(solution)/shard_map/ppermute | solution.py:531
  46.5 0.0 copy-done.1
  46.5 0.0 copy-done.3
  46.5 18.7 %field.1 = (f32[256,512]{1,0:T(8,128)}, f32[3,8192]{1,0:T(4,128)}) custom-call(s32[2]{0:T(128)S(1)} %pad_add_fusion.pos, s32[3,8192]{1,0:T(4,128)S(1)} %copy-done.1, f32[1,8192]{1,0:T(1,128)S(1)} %bitcast.7, f32[168,512]{1,0:T(8,128)S(1)} %get-tuple-element.19.down, f32[168,512]{1,0:T(8,128)S(1)} %get-tuple-element.20.up, ...), custom_call_target="tpu_custom_call" | custom-call | tf_op jit(solution)/shard_map/field/pallas_call | solution.py:601
Async XLA Ops:
  0.7 0.9 %copy-start = (s32[3,8192]{1,0:T(4,128)S(1)}, s32[3,8192]{1,0:T(4,128)}, u32[]{:S(2)}) copy-start(s32[3,8192]{1,0:T(4,128)} %cell.3) | copy-start | bytes 294916
  1.6 0.8 %copy-start.2 = (f32[8192]{0:T(1024)S(1)}, f32[8192]{0:T(1024)}, u32[]{:S(2)}) copy-start(f32[8192]{0:T(1024)} %param.4) | copy-start | bytes 98308
  2.4 44.1 %copy-start.1 = (s32[3,8192]{1,0:T(4,128)S(1)}, s32[3,8192]{1,0:T(4,128)}, u32[]{:S(2)}) copy-start(s32[3,8192]{1,0:T(4,128)} %cell.3) | copy-start | bytes 294916
  2.4 44.1 %copy-start.3 = (f32[8192]{0:T(1024)S(1)}, f32[8192]{0:T(1024)}, u32[]{:S(2)}) copy-start(f32[8192]{0:T(1024)} %param.4) | copy-start | bytes 98308
  9.3 28.9 %collective-permute-start.1 = (f32[168,512]{1,0:T(8,128)S(1)}, f32[168,512]{1,0:T(8,128)S(1)}, u32[]{:S(2)}, u32[]{:S(2)}) collective-permute-start(f32[168,512]{1,0:T(8,128)S(1)} %get-tuple-element.19.down), channel_id=1, source_target_pairs={{0,252},{1,253},{2,254},{3,255},{4,0},{5,1},{6,2},{7,3},{8,4},{9,5... | collective-permute-start | bytes 1032200 | tf_op jit(solution)/shard_map/ppermute | solution.py:531
  16.9 21.3 %collective-permute-start = (f32[168,512]{1,0:T(8,128)S(1)}, f32[168,512]{1,0:T(8,128)S(1)}, u32[]{:S(2)}, u32[]{:S(2)}) collective-permute-start(f32[168,512]{1,0:T(8,128)S(1)} %get-tuple-element.20.up), channel_id=1, source_target_pairs={{0,4},{1,5},{2,6},{3,7},{4,8},{5,9},{6,10},{7,11},{8,12},{9,13},{1... | collective-permute-start | bytes 1032200 | tf_op jit(solution)/shard_map/ppermute | solution.py:531
  16.9 24.0 %all-to-all-start = ((f32[256,2,128]{2,1,0:T(2,128)}), f32[256,2,128]{2,1,0:T(2,128)S(1)}, u32[]{:S(2)}, u32[]{:S(2)}) async-start(f32[256,2,128]{2,1,0:T(2,128)} %get-tuple-element.25), calls=%async_computation | async-start | bytes 524288 | tf_op jit(solution)/shard_map/all_to_all | solution.py:574
  26.9 11.3 %collective-permute-start.2 = (f32[8,128]{1,0:T(8,128)S(1)}, f32[8,128]{1,0:T(8,128)S(1)}, u32[]{:S(2)}, u32[]{:S(2)}) collective-permute-start(f32[8,128]{1,0:T(8,128)S(1)} %get-tuple-element.21), channel_id=1, source_target_pairs={{0,8},{1,9},{2,10},{3,11},{4,12},{5,13},{6,14},{7,15},{8,16},{9,17... | collective-permute-start | bytes 12296 | tf_op jit(solution)/shard_map/ppermute | solution.py:531
  28.4 9.7 %collective-permute-start.3 = (f32[8,128]{1,0:T(8,128)S(1)}, f32[8,128]{1,0:T(8,128)S(1)}, u32[]{:S(2)}, u32[]{:S(2)}) collective-permute-start(f32[8,128]{1,0:T(8,128)S(1)} %get-tuple-element.22), channel_id=1, source_target_pairs={{0,248},{1,249},{2,250},{3,251},{4,252},{5,253},{6,254},{7,255},{8... | collective-permute-start | bytes 12296 | tf_op jit(solution)/shard_map/ppermute | solution.py:531
  38.8 6.2 %collective-permute-start.4 = (f32[96,512]{1,0:T(8,128)S(1)}, f32[96,512]{1,0:T(8,128)S(1)}, u32[]{:S(2)}, u32[]{:S(2)}) collective-permute-start(f32[96,512]{1,0:T(8,128)S(1)} %get-tuple-element.23), channel_id=1, source_target_pairs={{0,1},{1,2},{2,3},{3,0},{4,5},{5,6},{6,7},{7,4},{8,9},{9,10},{10,1... | collective-permute-start | bytes 589832 | tf_op jit(solution)/shard_map/ppermute | solution.py:531
  39.2 7.3 %collective-permute-start.5 = (f32[96,512]{1,0:T(8,128)S(1)}, f32[96,512]{1,0:T(8,128)S(1)}, u32[]{:S(2)}, u32[]{:S(2)}) collective-permute-start(f32[96,512]{1,0:T(8,128)S(1)} %get-tuple-element.24), channel_id=1, source_target_pairs={{0,3},{1,0},{2,1},{3,2},{4,7},{5,4},{6,5},{7,6},{8,11},{9,8},{10,9... | collective-permute-start | bytes 589832 | tf_op jit(solution)/shard_map/ppermute | solution.py:531

commit v5 on v4

--- a/solution.py
+++ b/solution.py
@@ -400,8 +400,8 @@
 def field_kernel(
     pos, cell, charge, down, up, below, above, far_below, far_above, left, right, coarse,
     w0, w1, w2, d1, d2, uz, uy,
-    potential_hbm, forces_hbm,
-    potential, forces, high0, low0, high1, low1, high2, low2, fields, weights, wide1, wide2, grid, slopes, sems,
+    potential_hbm, forces,
+    potential, high0, low0, high1, low1, high2, low2, fields, weights, wide1, wide2, grid, slopes, sems,
 ):
     slab = pos[0]
     pencil = pos[1]
@@ -496,7 +496,6 @@
 
     put = pltpu.make_async_copy(potential, potential_hbm, sems.at[0])
     put.start()
-    puts = [put]
 
     for block in range(ATOMS_DEV // BLOCK_B):
         at = slice(block * BLOCK_B, block * BLOCK_B + BLOCK_B)
@@ -512,10 +511,7 @@
                 left = [jnp.where(bit, left[2 * i + 1], left[2 * i]) for i in range(len(left) // 2)]
             picked = jnp.sum(jnp.where(last, left[0], 0.0), axis=0, keepdims=True)
             forces[d : d + 1, at] = -charge[0:1, at] * picked
-        puts.append(pltpu.make_async_copy(forces.at[:, at], forces_hbm.at[:, at], sems.at[1 + block]))
-        puts[-1].start()
-    for put in puts:
-        put.wait()
+    put.wait()
 
 
 def specs(*spaces):
@@ -602,10 +598,9 @@
             field_kernel,
             out_shape=(f32_shape(CZ * CY, NX), f32_shape(3, ATOMS_DEV)),
             in_specs=specs((pltpu.SMEM, 1), (pltpu.VMEM, 18)),
-            out_specs=specs((pltpu.HBM, 2)),
+            out_specs=specs((pltpu.HBM, 1), (pltpu.VMEM, 1)),
             scratch_shapes=[
                 pltpu.VMEM((CZ * CY, NX), F32),
-                pltpu.VMEM((3, ATOMS_DEV), F32),
                 pltpu.VMEM((768, NX), BF),
                 pltpu.VMEM((768, NX), BF),
                 pltpu.VMEM((384, 256), BF),
@@ -618,7 +613,7 @@
                 pltpu.VMEM((64, 384), F32),
                 pltpu.VMEM((480, NX), F32),
                 pltpu.VMEM((768, 1024), BF),
-                pltpu.SemaphoreType.DMA((1 + ATOMS_DEV // BLOCK_B,)),
+                pltpu.SemaphoreType.DMA((1,)),
             ],
             compiler_params=pltpu.CompilerParams(vmem_limit_bytes=40 * 2**20),
             name="field",

time: 65.6 us -> 65.7 us (level)
  no operation moved by 1% of the time
where the time goes in v5:
time: 65.7 us; the launch traced here: 65.4 us
  Pallas kernels  28.9 us (44%)
  starting transfers between devices  26.5 us (40%)
  waiting for transfers between devices  7.39 us (11%)
  local copies, waits for them, and re-layouts  1.67 us (3%)
  between operations  0.84 us (1%)
    pallas_call x1, Pallas kernels, body(): pl.pallas_call(field_kernel, out_shape=(f32_shape(CZ * CY, NX), f32_shape...  18.7 us
    ppermute x6, starting transfers between devices, rotated(): return lax.ppermute(value, BOTH, pairs)  16.6 us
    all_to_all x1, starting transfers between devices, body(): level3 = lax.all_to_all(copies, BOTH, 0, 0, tiled=True).reshape(512, 128)  9.97 us
    ppermute x6, waiting for transfers between devices, rotated(): return lax.ppermute(value, BOTH, pairs)  7.39 us
    pallas_call x1, Pallas kernels, body(): pl.pallas_call(partial(deposit_kernel, blocks('block_sums', 'sums')), out...  6.95 us
    pallas_call x1, Pallas kernels, body(): pl.pallas_call(partial(coarse_kernel, blocks(*wanted), blocks(*later), pl...  2.63 us
    unnamed x8, local copies, waits for them, and re-layouts  1.67 us
  transfers between devices with their start and end apart: 7, of which 3 were waited for; matrix products, arithmetic and copies ran while one was open for 0% of the time, Pallas kernels for 5%

profile of v5, /device:TPU:24, one launch (start us, length us, event | category | flops | bytes accessed | tf_op | source)
XLA Modules:
  0.0 65.4 jit_solution(1347228572498830689)
XLA Ops:
  0.6 0.1 pad_add_fusion.pos
  0.7 0.0 copy-start
  0.7 0.9 %copy-done = s32[3,8192]{1,0:T(4,128)S(1)} copy-done((s32[3,8192]{1,0:T(4,128)S(1)}, s32[3,8192]{1,0:T(4,128)}, u32[]{:S(2)}) %copy-start) | copy-done | bytes 98328
  1.6 0.0 copy-start.2
  1.6 0.8 %copy-done.2 = f32[8192]{0:T(1024)S(1)} copy-done((f32[8192]{0:T(1024)S(1)}, f32[8192]{0:T(1024)}, u32[]{:S(2)}) %copy-start.2) | copy-done | bytes 32792
  2.4 0.0 copy-start.1
  2.4 0.0 copy-start.3
  2.4 6.9 %deposit.1 = (f32[168,512]{1,0:T(8,128)S(1)}, f32[168,512]{1,0:T(8,128)S(1)}, f32[8,128]{1,0:T(8,128)S(1)}, f32[8,128]{1,0:T(8,128)S(1)}, f32[256,2,128]{2,1,0:T(2,128)}) custom-call(s32[2]{0:T(128)S(1)} %pad_add_fusion.pos, s32[3,8192]{1,0:T(4,128)S(1)} %copy-done, f32[1,8192]{1,0:T(1,128)S(1)} %bitcast.6, bf16[28672,512]{1,0:T(8,128)(2,1)} %constant.11.clone.bank), custom_call_target="tpu_custom_call" | custom-call | tf_op jit(solution)/shard_map/deposit/pallas_call | solution.py:552
  9.3 7.6 %collective-permute-start.1 = (f32[168,512]{1,0:T(8,128)S(1)}, f32[168,512]{1,0:T(8,128)S(1)}, u32[]{:S(2)}, u32[]{:S(2)}) collective-permute-start(f32[168,512]{1,0:T(8,128)S(1)} %get-tuple-element.19.down), channel_id=1, source_target_pairs={{0,252},{1,253},{2,254},{3,255},{4,0},{5,1},{6,2},{7,3},{8,4},{9,5... | collective-permute-start | bytes 1032200 | tf_op jit(solution)/shard_map/ppermute | solution.py:527
  16.9 0.0 collective-permute-start
  16.9 10.0 %all-to-all-start = ((f32[256,2,128]{2,1,0:T(2,128)}), f32[256,2,128]{2,1,0:T(2,128)S(1)}, u32[]{:S(2)}, u32[]{:S(2)}) async-start(f32[256,2,128]{2,1,0:T(2,128)} %get-tuple-element.25), calls=%async_computation | async-start | bytes 524288 | tf_op jit(solution)/shard_map/all_to_all | solution.py:570
  26.9 1.6 %collective-permute-start.2 = (f32[8,128]{1,0:T(8,128)S(1)}, f32[8,128]{1,0:T(8,128)S(1)}, u32[]{:S(2)}, u32[]{:S(2)}) collective-permute-start(f32[8,128]{1,0:T(8,128)S(1)} %get-tuple-element.21), channel_id=1, source_target_pairs={{0,8},{1,9},{2,10},{3,11},{4,12},{5,13},{6,14},{7,15},{8,16},{9,17... | collective-permute-start | bytes 12296 | tf_op jit(solution)/shard_map/ppermute | solution.py:527
  28.4 5.3 %collective-permute-start.3 = (f32[8,128]{1,0:T(8,128)S(1)}, f32[8,128]{1,0:T(8,128)S(1)}, u32[]{:S(2)}, u32[]{:S(2)}) collective-permute-start(f32[8,128]{1,0:T(8,128)S(1)} %get-tuple-element.22), channel_id=1, source_target_pairs={{0,248},{1,249},{2,250},{3,251},{4,252},{5,253},{6,254},{7,255},{8... | collective-permute-start | bytes 12296 | tf_op jit(solution)/shard_map/ppermute | solution.py:527
  33.8 4.4 %collective-permute-done.2.far_below = f32[8,128]{1,0:T(8,128)S(1)} collective-permute-done((f32[8,128]{1,0:T(8,128)S(1)}, f32[8,128]{1,0:T(8,128)S(1)}, u32[]{:S(2)}, u32[]{:S(2)}) %collective-permute-start.2) | collective-permute-done | bytes 4128 | tf_op jit(solution)/shard_map/ppermute | solution.py:527
  38.2 0.0 collective-permute-done.3.far_above
  38.2 0.0 collective-permute-done.1.above
  38.2 0.0 collective-permute-done.below
  38.2 0.6 pack.1
  38.8 0.4 collective-permute-start.4
  39.2 1.7 %collective-permute-start.5 = (f32[96,512]{1,0:T(8,128)S(1)}, f32[96,512]{1,0:T(8,128)S(1)}, u32[]{:S(2)}, u32[]{:S(2)}) collective-permute-start(f32[96,512]{1,0:T(8,128)S(1)} %get-tuple-element.24), channel_id=1, source_target_pairs={{0,3},{1,0},{2,1},{3,2},{4,7},{5,4},{6,5},{7,6},{8,11},{9,8},{10,9... | collective-permute-start | bytes 589832 | tf_op jit(solution)/shard_map/ppermute | solution.py:527
  40.9 0.0 all-to-all-done
  40.9 2.6 %coarse.1 = (f32[128,512]{1,0:T(8,128)S(1)}, bf16[256,256]{1,0:T(8,128)(2,1)S(1)}, bf16[160,256]{1,0:T(8,128)(2,1)S(1)}, bf16[96,256]{1,0:T(8,128)(2,1)S(1)}, bf...) custom-call(s32[2]{0:T(128)S(1)} %pad_add_fusion.pos, ...), custom_call_target="tpu_custom_call" | custom-call | tf_op jit(solution)/shard_map/coarse/pallas_call | solution.py:583
  43.5 1.5 %collective-permute-done.4.left = f32[96,512]{1,0:T(8,128)S(1)} collective-permute-done((f32[96,512]{1,0:T(8,128)S(1)}, f32[96,512]{1,0:T(8,128)S(1)}, u32[]{:S(2)}, u32[]{:S(2)}) %collective-permute-start.4) | collective-permute-done | bytes 196640 | tf_op jit(solution)/shard_map/ppermute | solution.py:527
  45.0 1.5 %collective-permute-done.5.right = f32[96,512]{1,0:T(8,128)S(1)} collective-permute-done((f32[96,512]{1,0:T(8,128)S(1)}, f32[96,512]{1,0:T(8,128)S(1)}, u32[]{:S(2)}, u32[]{:S(2)}) %collective-permute-start.5) | collective-permute-done | bytes 196640 | tf_op jit(solution)/shard_map/ppermute | solution.py:527
  46.5 0.0 copy-done.1
  46.5 0.0 copy-done.3
  46.5 18.7 %field.1 = (f32[256,512]{1,0:T(8,128)}, f32[3,8192]{1,0:T(4,128)}) custom-call(s32[2]{0:T(128)S(1)} %pad_add_fusion.pos, s32[3,8192]{1,0:T(4,128)S(1)} %copy-done.1, f32[1,8192]{1,0:T(1,128)S(1)} %bitcast.7, f32[168,512]{1,0:T(8,128)S(1)} %get-tuple-element.19.down, f32[168,512]{1,0:T(8,128)S(1)} %get-tuple-element.20.up, ...), custom_call_target="tpu_custom_call" | custom-call | tf_op jit(solution)/shard_map/field/pallas_call | solution.py:597
Async XLA Ops:
  0.7 0.9 %copy-start = (s32[3,8192]{1,0:T(4,128)S(1)}, s32[3,8192]{1,0:T(4,128)}, u32[]{:S(2)}) copy-start(s32[3,8192]{1,0:T(4,128)} %cell.3) | copy-start | bytes 294916
  1.6 0.8 %copy-start.2 = (f32[8192]{0:T(1024)S(1)}, f32[8192]{0:T(1024)}, u32[]{:S(2)}) copy-start(f32[8192]{0:T(1024)} %param.4) | copy-start | bytes 98308
  2.4 44.1 %copy-start.1 = (s32[3,8192]{1,0:T(4,128)S(1)}, s32[3,8192]{1,0:T(4,128)}, u32[]{:S(2)}) copy-start(s32[3,8192]{1,0:T(4,128)} %cell.3) | copy-start | bytes 294916
  2.4 44.1 %copy-start.3 = (f32[8192]{0:T(1024)S(1)}, f32[8192]{0:T(1024)}, u32[]{:S(2)}) copy-start(f32[8192]{0:T(1024)} %param.4) | copy-start | bytes 98308
  9.3 28.9 %collective-permute-start.1 = (f32[168,512]{1,0:T(8,128)S(1)}, f32[168,512]{1,0:T(8,128)S(1)}, u32[]{:S(2)}, u32[]{:S(2)}) collective-permute-start(f32[168,512]{1,0:T(8,128)S(1)} %get-tuple-element.19.down), channel_id=1, source_target_pairs={{0,252},{1,253},{2,254},{3,255},{4,0},{5,1},{6,2},{7,3},{8,4},{9,5... | collective-permute-start | bytes 1032200 | tf_op jit(solution)/shard_map/ppermute | solution.py:527
  16.9 21.3 %collective-permute-start = (f32[168,512]{1,0:T(8,128)S(1)}, f32[168,512]{1,0:T(8,128)S(1)}, u32[]{:S(2)}, u32[]{:S(2)}) collective-permute-start(f32[168,512]{1,0:T(8,128)S(1)} %get-tuple-element.20.up), channel_id=1, source_target_pairs={{0,4},{1,5},{2,6},{3,7},{4,8},{5,9},{6,10},{7,11},{8,12},{9,13},{1... | collective-permute-start | bytes 1032200 | tf_op jit(solution)/shard_map/ppermute | solution.py:527
  16.9 24.0 %all-to-all-start = ((f32[256,2,128]{2,1,0:T(2,128)}), f32[256,2,128]{2,1,0:T(2,128)S(1)}, u32[]{:S(2)}, u32[]{:S(2)}) async-start(f32[256,2,128]{2,1,0:T(2,128)} %get-tuple-element.25), calls=%async_computation | async-start | bytes 524288 | tf_op jit(solution)/shard_map/all_to_all | solution.py:570
  26.9 11.3 %collective-permute-start.2 = (f32[8,128]{1,0:T(8,128)S(1)}, f32[8,128]{1,0:T(8,128)S(1)}, u32[]{:S(2)}, u32[]{:S(2)}) collective-permute-start(f32[8,128]{1,0:T(8,128)S(1)} %get-tuple-element.21), channel_id=1, source_target_pairs={{0,8},{1,9},{2,10},{3,11},{4,12},{5,13},{6,14},{7,15},{8,16},{9,17... | collective-permute-start | bytes 12296 | tf_op jit(solution)/shard_map/ppermute | solution.py:527
  28.4 9.7 %collective-permute-start.3 = (f32[8,128]{1,0:T(8,128)S(1)}, f32[8,128]{1,0:T(8,128)S(1)}, u32[]{:S(2)}, u32[]{:S(2)}) collective-permute-start(f32[8,128]{1,0:T(8,128)S(1)} %get-tuple-element.22), channel_id=1, source_target_pairs={{0,248},{1,249},{2,250},{3,251},{4,252},{5,253},{6,254},{7,255},{8... | collective-permute-start | bytes 12296 | tf_op jit(solution)/shard_map/ppermute | solution.py:527
  38.8 6.2 %collective-permute-start.4 = (f32[96,512]{1,0:T(8,128)S(1)}, f32[96,512]{1,0:T(8,128)S(1)}, u32[]{:S(2)}, u32[]{:S(2)}) collective-permute-start(f32[96,512]{1,0:T(8,128)S(1)} %get-tuple-element.23), channel_id=1, source_target_pairs={{0,1},{1,2},{2,3},{3,0},{4,5},{5,6},{6,7},{7,4},{8,9},{9,10},{10,1... | collective-permute-start | bytes 589832 | tf_op jit(solution)/shard_map/ppermute | solution.py:527
  39.2 7.3 %collective-permute-start.5 = (f32[96,512]{1,0:T(8,128)S(1)}, f32[96,512]{1,0:T(8,128)S(1)}, u32[]{:S(2)}, u32[]{:S(2)}) collective-permute-start(f32[96,512]{1,0:T(8,128)S(1)} %get-tuple-element.24), channel_id=1, source_target_pairs={{0,3},{1,0},{2,1},{3,2},{4,7},{5,4},{6,5},{7,6},{8,11},{9,8},{10,9... | collective-permute-start | bytes 589832 | tf_op jit(solution)/shard_map/ppermute | solution.py:527
